TPU v7x, 32 devices: a whole 2x2x4 slice. The times are simulated.
32 devices in a mesh: wide: 8 (over z, x), narrow: 4 (over y, core).
Axes of the slice: x: 2, y: 2, z: 4, core: 2. Of those that a mesh axis runs over, the one named last changes fastest.
Arguments:
- object_field: float32 [2, 2048, 2048], P(None, 'narrow', 'wide'), may hold values from -6 to 6
- probe: float32 [4, 2, 256, 256], replicated, may hold values from -3 to 3
- amplitudes: float32 [256, 256, 256], P(('wide', 'narrow')), may hold values from 0.5 to 4
- offsets: int32 [256, 2], P(('wide', 'narrow')), may hold values from 0 to 1792, as said below
- live: int32 [32], P(('wide', 'narrow')), may hold values from 1 to 8, as said below
Outputs:
- object_grad: float32 [2, 2048, 2048], P(None, 'narrow', 'wide')
- probe_grad: float32 [4, 2, 256, 256], replicated
Inputs may be any that keep to these rules, and one draw needn't show every extreme that they name: `offsets`: the patch of every slot (used or not) lies wholly inside the object, and starts inside the object tile of 512 rows and 256 columns that holds the same mesh place as the slot: slot p with b = p // 8, row tile b % (2048 / 512) and column tile b // (2048 / 512). Block b of 8 slots uses its first live[b] slots; in every draw some block uses all 8.
All inputs are finite; a program needn't handle non-finite values.
Results may differ from a plain program's by a relative error of at most 0.005.
Values sent between devices are 32-bit elements; how exact they have to be, the bound alone decides.
No kernel may reach another device: no remote copies, remote signals or barrier semaphores. Data moves between devices by JAX's collectives and lax.ppermute only.
A program may use at most 128 MiB of HBM per device.

v0:
```python
import functools
import math

import jax
import jax.numpy as jnp
import ml_dtypes
import numpy as np
from jax import lax
from jax.experimental import pallas as pl
from jax.experimental.pallas import tpu as pltpu
from jax.sharding import PartitionSpec as P

F32 = jnp.float32
BF16 = jnp.bfloat16
LANES = 128


def half_dft(extent):
    half = extent // 2
    blocks = []
    for parity in range(2):
        freq = 2 * np.arange(half)[:, None] + parity
        angles = (freq * np.arange(half)[None, :] % extent) * (2.0 * math.pi / extent)
        cosine = np.cos(angles) / math.sqrt(extent)
        sine = np.sin(angles) / math.sqrt(extent)
        blocks.append(np.block([[cosine, sine], [-sine, cosine]]))
    both = np.stack(blocks)
    return np.stack([both, np.swapaxes(both, 1, 2)]).astype(ml_dtypes.bfloat16)


def parity_order(extent):
    order = np.concatenate([np.arange(0, extent, 2), np.arange(1, extent, 2)])
    matrix = np.zeros((extent, extent), np.float32)
    matrix[order, np.arange(extent)] = 1.0
    return matrix


def dot(a, b):
    return jnp.dot(a, b, preferred_element_type=F32)


def slots_kernel(
    tile_rows, tile_cols, offsets, live, own, below, right, right_low, corner, probe_in, amps, mats, order,
    grad_own, grad_below, grad_right, grad_right_low, grad_corner, probe_keep, probe_send,
    ext, grad, probe, probe_sum, window, part, amp, sorted_amp, waves, inner, far, power, across,
    in_sems, amp_sem, out_sems,
):
    modes = probe.shape[0]
    extent = probe.shape[2]
    half = extent // 2
    rows_step = 32
    groups = rows_step // 8
    count = live[0]

    low_rows = slice(tile_rows, tile_rows + extent)
    whole = slice(0, tile_cols)
    rim = slice(tile_cols, tile_cols + extent)
    places = [
        (own, slice(0, tile_rows), whole),
        (below, low_rows, whole),
        (right, slice(0, extent), rim),
        (right_low, slice(extent, tile_rows), rim),
        (corner, low_rows, rim),
    ]
    loads = [
        pltpu.make_async_copy(src, ext.at[:, rows, cols], in_sems.at[n])
        for n, (src, rows, cols) in enumerate(places)
    ]
    loads.append(pltpu.make_async_copy(probe_in, probe, in_sems.at[len(places)]))
    for load in loads:
        load.start()
    grad[...] = jnp.zeros_like(grad)
    probe_sum[...] = jnp.zeros_like(probe_sum)
    for load in loads:
        load.wait()
    lane = lax.broadcasted_iota(jnp.int32, (rows_step, LANES), 1)
    lane3 = lax.broadcasted_iota(jnp.int32, (groups + 1, 8, LANES), 2)
    sublane = lax.broadcasted_iota(jnp.int32, (groups, 8, LANES), 1)
    sublane_tall = lax.broadcasted_iota(jnp.int32, (groups + 1, 8, LANES), 1)

    def rows_of(k, c, rows):
        start = (k * 2 + c) * extent
        return slice(start + rows.start, start + rows.stop)

    def visit(number, row_at, col_at):
        amp_load = pltpu.make_async_copy(amps.at[number], amp, amp_sem)
        amp_load.start()
        shift = lax.rem(col_at, LANES)
        col_base = pl.multiple_of(col_at - shift, LANES)
        back = lax.rem(LANES - shift, LANES)
        wide_cols = extent // LANES + 1
        row_shift = lax.rem(row_at, 8)
        row_base = pl.multiple_of(row_at - row_shift, 8)
        row_back = lax.rem(8 - row_shift, 8)

        for plane in range(2):
            for row in range(0, extent, rows_step):
                turned = []
                for c in range(wide_cols):
                    tall = ext[plane, pl.ds(row_base + row, rows_step + 8), pl.ds(col_base + LANES * c, LANES)]
                    tall = pltpu.roll(tall.reshape(groups + 1, 8, LANES), row_back, 1)
                    flat = jnp.where(sublane < 8 - row_shift, tall[:-1], tall[1:]).reshape(rows_step, LANES)
                    turned.append(pltpu.roll(flat, back, 1))
                for c in range(wide_cols - 1):
                    window[plane, row : row + rows_step, c * LANES : (c + 1) * LANES] = jnp.where(
                        lane < LANES - shift, turned[c], turned[c + 1]
                    )


        def psi(k, step=rows_step):
            for row in range(0, half, step):
                waves_at = []
                for base in (row, half + row):
                    rows = slice(base, base + step)
                    pr, pi = probe[k, 0, rows, :], probe[k, 1, rows, :]
                    o_re, o_im = window[0, rows, :], window[1, rows, :]
                    waves_at.append((pr * o_re - pi * o_im, pr * o_im + pi * o_re))
                for c in range(2):
                    rows = slice(c * half + row, c * half + row + step)
                    waves[k, 0, rows, :] = (waves_at[0][c] + waves_at[1][c]).astype(BF16)
                    waves[k, 1, rows, :] = (waves_at[0][c] - waves_at[1][c]).astype(BF16)

        def left(k):
            for a in range(2):
                z = dot(mats[0, a], waves[k, a])
                left, right_half = z[:, :half], z[:, half:]
                for b, value in enumerate((left + right_half, left - right_half)):
                    value = value.astype(BF16)
                    inner[k, b, a * half : (a + 1) * half, :half] = value[:half]
                    inner[k, b, a * half : (a + 1) * half, half:] = value[half:]

        def right(k):
            for b in range(2):
                f = dot(inner[k, b], mats[1, b])
                far[k, b] = f
                own_power = f[:, :half] * f[:, :half] + f[:, half:] * f[:, half:]
                power[b] = own_power if k == 0 else power[b] + own_power

        def factors():
            amp_load.wait()
            high = amp[...].astype(BF16)
            low = (amp[...] - high.astype(F32)).astype(BF16)
            turned = dot(high, order[...]) + dot(low, order[...])
            for b in range(2):
                sorted_amp[b] = turned[:, b * half : (b + 1) * half]
            for b in range(2):
                for a in range(2):
                    rows = slice(a * half, (a + 1) * half)
                    for_rows = sorted_amp[b, pl.ds(a, half, 2), :]
                    power[b, rows] = 2.0 - 2.0 * for_rows * lax.rsqrt(power[b, rows] + 0.5)

        def back_right(k):
            ys = []
            for b in range(2):
                factor = power[b]
                g = jnp.concatenate([far[k, b, :, :half] * factor, far[k, b, :, half:] * factor], 1)
                ys.append(dot(g.astype(BF16), mats[0, b]))
            for side, y in enumerate((ys[0] + ys[1], ys[0] - ys[1])):
                y = y.astype(BF16)
                cols = slice(side * half, (side + 1) * half)
                for a in range(2):
                    rows = slice(a * half, (a + 1) * half)
                    across[k, a, :half, cols] = y[rows, :half]
                    across[k, a, half:, cols] = y[rows, half:]

        def back_left(k):
            v0 = dot(mats[1, 0], across[k, 0])
            v1 = dot(mats[1, 1], across[k, 1])
            for side, v in enumerate((v0 + v1, v0 - v1)):
                rows = slice(side * half, (side + 1) * half)
                g_re, g_im = v[:half], v[half:]
                pr, pi = probe[k, 0, rows, :], probe[k, 1, rows, :]
                o_re, o_im = window[0, rows, :], window[1, rows, :]
                add_re = pr * g_re + pi * g_im
                add_im = pr * g_im - pi * g_re
                part[0, rows, :] = add_re if k == 0 else part[0, rows, :] + add_re
                part[1, rows, :] = add_im if k == 0 else part[1, rows, :] + add_im
                probe_sum[rows_of(k, 0, rows), :] += o_re * g_re + o_im * g_im
                probe_sum[rows_of(k, 1, rows), :] += o_re * g_im - o_im * g_re

        for stage in (psi, left, right):
            for k in range(modes):
                stage(k)
        factors()
        for stage in (back_right, back_left):
            for k in range(modes):
                stage(k)

        zero = jnp.zeros((groups + 1, 8, LANES), F32)
        edge = jnp.zeros((1, 8, LANES), F32)
        for plane in range(2):
            for row in range(0, extent, rows_step):
                turned = []
                for c in range(wide_cols - 1):
                    flat = part[plane, row : row + rows_step, c * LANES : (c + 1) * LANES]
                    flat = pltpu.roll(flat, shift, 1).reshape(groups, 8, LANES)
                    flat = pltpu.roll(flat, row_shift, 1)
                    low = jnp.concatenate([flat, edge], 0)
                    high = jnp.concatenate([edge, flat], 0)
                    turned.append(jnp.where(sublane_tall >= row_shift, low, high))
                turned = [zero] + turned + [zero]
                for c in range(wide_cols):
                    at = (plane, pl.ds(row_base + row, rows_step + 8), pl.ds(col_base + LANES * c, LANES))
                    value = jnp.where(lane3 >= shift, turned[c + 1], turned[c])
                    grad[at] += value.reshape(rows_step + 8, LANES)

    @pl.loop(0, count)
    def _(number):
        row_at = lax.rem(offsets[number, 0], tile_rows)
        col_at = lax.rem(offsets[number, 1], tile_cols)

        visit(number, row_at, col_at)

    own_half = (lax.axis_index("narrow") & 1) * (probe_sum.shape[0] // 2)
    other_half = probe_sum.shape[0] // 2 - own_half
    pairs = [
        (probe_sum.at[pl.ds(pl.multiple_of(start, 8), probe_sum.shape[0] // 2), :], dst)
        for start, dst in ((other_half, probe_send), (own_half, probe_keep))
    ] + [
        (grad.at[:, low_rows, rim], grad_corner),
        (grad.at[:, low_rows, whole], grad_below),
        (grad.at[:, 0:extent, rim], grad_right),
        (grad.at[:, extent:tile_rows, rim], grad_right_low),
        (grad.at[:, 0:tile_rows, whole], grad_own),
    ]
    stores = [pltpu.make_async_copy(src, dst, out_sems.at[n]) for n, (src, dst) in enumerate(pairs)]
    for store in stores:
        store.start()
    for store in stores:
        store.wait()


def run_slots(offsets, live, own, below, right, right_low, corner, probe, amps):
    extent = probe.shape[2]
    modes = probe.shape[0]
    tile_rows, tile_cols = own.shape[1:]
    mats = jnp.asarray(half_dft(extent))
    order = jnp.asarray(parity_order(extent)).astype(BF16)
    smem = pl.BlockSpec(memory_space=pltpu.SMEM)
    vmem = pl.BlockSpec(memory_space=pltpu.VMEM)
    hbm = pl.BlockSpec(memory_space=pl.ANY)
    grad_shape = (2, tile_rows + extent, tile_cols + extent)
    sum_shape = (modes * 2 * extent, extent)
    half_sum = (sum_shape[0] // 2, extent)
    outs = [(2, tile_rows, tile_cols), (2, extent, tile_cols), (2, extent, extent), (2, tile_rows - extent, extent)]
    outs += [(2, extent, extent), half_sum, half_sum]
    return pl.pallas_call(
        functools.partial(slots_kernel, tile_rows, tile_cols),
        out_shape=[jax.ShapeDtypeStruct(shape, F32) for shape in outs],
        in_specs=[smem, smem] + [hbm] * 7 + [vmem, vmem],
        out_specs=[hbm] * len(outs),
        scratch_shapes=[
            pltpu.VMEM(grad_shape, F32),
            pltpu.VMEM(grad_shape, F32),
            pltpu.VMEM(probe.shape, F32),
            pltpu.VMEM(sum_shape, F32),
            pltpu.VMEM((2, extent, extent), F32),
            pltpu.VMEM((2, extent, extent), F32),
            pltpu.VMEM((extent, extent), F32),
            pltpu.VMEM((2, extent, extent // 2), F32),
            pltpu.VMEM((modes, 2, extent, extent), BF16),
            pltpu.VMEM((modes, 2, extent, extent), BF16),
            pltpu.VMEM((modes, 2, extent, extent), F32),
            pltpu.VMEM((2, extent, extent // 2), F32),
            pltpu.VMEM((modes, 2, extent, extent), BF16),
            pltpu.SemaphoreType.DMA((6,)),
            pltpu.SemaphoreType.DMA(()),
            pltpu.SemaphoreType.DMA((7,)),
        ],
        compiler_params=pltpu.CompilerParams(vmem_limit_bytes=60 * 1024 * 1024),
        name="slots",
    )(offsets, live, own, below, right, right_low, corner, probe, amps, mats, order)


def shifted(value, axis, steps):
    count = lax.axis_size(axis)
    first, last = (max(0, -steps), min(count, count - steps))
    return lax.ppermute(value, axis, [(source, source + steps) for source in range(first, last)])


def place_in(bits):
    linear = lax.axis_index("wide") * lax.axis_size("narrow") + lax.axis_index("narrow")
    place = 0
    for n, bit in enumerate(bits):
        place = place + ((linear // bit) % 2) * (1 << n)
    return place


def partners(bits):
    return [sum(bit for n, bit in enumerate(bits) if step >> n & 1) for step in range(1 << len(bits))]


def swapped(value, mask):
    count = lax.axis_size("wide") * lax.axis_size("narrow")
    return lax.ppermute(value, ("wide", "narrow"), [(source, source ^ mask) for source in range(count)])


def add_kernel(bits, count, *refs):
    ins, outs = refs[:count], refs[count:]
    rows = outs[0].shape[0]
    place = place_in(bits)
    for step, out in enumerate(outs):
        at = pl.ds(pl.multiple_of((place ^ step) * rows, 8), rows)
        out[...] = sum(ref[at, :] for ref in ins)


def add_parts(parts, bits):
    count = 1 << len(bits)
    rows, cols = parts[0].shape
    vmem = pl.BlockSpec(memory_space=pltpu.VMEM)
    return pl.pallas_call(
        functools.partial(add_kernel, bits, len(parts)),
        out_shape=[jax.ShapeDtypeStruct((rows // count, cols), F32)] * count,
        in_specs=[vmem] * len(parts),
        out_specs=[vmem] * count,
        compiler_params=pltpu.CompilerParams(vmem_limit_bytes=8 * 1024 * 1024),
        name="add_parts",
    )(*parts)


def join_kernel(bits, scale, *refs):
    ins, out = refs[:-1], refs[-1]
    rows = ins[0].shape[0]
    place = place_in(bits)
    for step, ref in enumerate(ins):
        at = pl.ds(pl.multiple_of((place ^ step) * rows, 8), rows)
        out[at, :] = ref[...] if scale is None else ref[...] * scale


def join_parts(parts, bits, scale=None):
    rows, cols = parts[0].shape
    vmem = pl.BlockSpec(memory_space=pltpu.VMEM)
    return pl.pallas_call(
        functools.partial(join_kernel, bits, scale),
        out_shape=jax.ShapeDtypeStruct((rows * len(parts), cols), F32),
        in_specs=[vmem] * len(parts),
        out_specs=vmem,
        compiler_params=pltpu.CompilerParams(vmem_limit_bytes=8 * 1024 * 1024),
        name="join_parts",
    )(*parts)


def sum_everywhere(keep, send, scale, beside):
    narrow, wide = lax.axis_size("narrow"), lax.axis_size("wide")
    bits = [1 << n for n in range((narrow * wide).bit_length() - 1)]
    groups = [tuple(bits[n : n + 2]) for n in range(1, len(bits), 2)]
    parts = [keep, swapped(send, bits[0])]
    for group in groups:
        pieces = add_parts(parts, group)
        parts = [pieces[0]] + [swapped(piece, mask) for piece, mask in zip(pieces[1:], partners(group)[1:])]
        if group == groups[0]:
            parts, beside = lax.optimization_barrier((parts, beside))
    value = add_parts(parts, ())[0]
    for group in reversed(groups):
        parts = [value] + [swapped(value, mask) for mask in partners(group)[1:]]
        if group != groups[0]:
            value = join_parts(parts, group)
    parts = parts + [swapped(part, bits[0]) for part in parts]
    return join_parts(parts, groups[0] + (bits[0],), scale), beside


def on_device(object_field, probe, amplitudes, offsets, live):
    extent = probe.shape[2]
    top = object_field[:, :extent]
    right = shifted(top, "wide", -1)
    below = shifted(top, "narrow", -1)
    right_low = shifted(object_field[:, extent:], "wide", -1)
    corner = shifted(right, "narrow", -1)
    grad_own, grad_below, grad_right, grad_right_low, grad_corner, keep, send = run_slots(
        offsets, live, object_field, below, right, right_low, corner, probe, amplitudes
    )
    grad_right, keep, send = lax.optimization_barrier((grad_right + shifted(grad_corner, "narrow", 1), keep, send))
    beside = [shifted(grad_below, "narrow", 1), shifted(grad_right, "wide", 1), shifted(grad_right_low, "wide", 1)]
    total_slots = lax.axis_size("wide") * lax.axis_size("narrow") * offsets.shape[0]
    probe_grad, beside = sum_everywhere(keep, send, 1.0 / math.sqrt(total_slots), beside)
    came_below, came_right, came_right_low = beside
    rims = jnp.concatenate([came_right, came_right_low], 1)
    object_grad = grad_own.at[:, :extent, :].add(came_below).at[:, :, :extent].add(rims)
    return (object_grad, probe_grad.reshape(probe.shape))


def solution(mesh):
    return jax.shard_map(
        on_device,
        mesh=mesh,
        in_specs=(
            P(None, "narrow", "wide"),
            P(),
            P(("wide", "narrow"), None, None),
            P(("wide", "narrow"), None),
            P(("wide", "narrow")),
        ),
        out_specs=(P(None, "narrow", "wide"), P()),
        check_vma=False,
    )
```

profile of v0, /device:TPU:0, one launch (start us, length us, event | category | flops | bytes accessed | tf_op | source)
XLA Modules:
  0.0 152.0 jit_solution(14438458046363855835)
XLA Ops:
  0.6 1.3 fusion
  1.9 1.3 collective-permute-start.1
  3.2 1.3 collective-permute-start
  4.5 1.3 collective-permute-start.2
  5.8 13.7 %collective-permute-done.1.right = f32[2,256,256]{2,1,0:T(8,128)S(1)} collective-permute-done((f32[2,256,256]{2,1,0:T(8,128)S(1)}, f32[2,256,256]{2,1,0:T(8,128)S(1)}, u32[]{:S(2)}, u32[]{:S(2)}) %collective-permute-start.1) | collective-permute-done | bytes 524320 | tf_op jit(solution)/shard_map/ppermute | solution.py:278
  19.5 1.3 collective-permute-start.3
  22.1 7.8 %collective-permute-done.2.right_low = f32[2,256,256]{2,1,0:T(8,128)S(1)} collective-permute-done((f32[2,256,256]{2,1,0:T(8,128)S(1)}, f32[2,256,256]{2,1,0:T(8,128)S(1)}, u32[]{:S(2)}, u32[]{:S(2)}) %collective-permute-start.2) | collective-permute-done | bytes 524320 | tf_op jit(solution)/shard_map/ppermute | solution.py:278
  31.7 9.4 %slots.1 = (f32[2,512,256]{2,1,0:T(8,128)}, f32[2,256,256]{2,1,0:T(8,128)}, f32[2,256,256]{2,1,0:T(8,128)}, f32[2,256,256]{2,1,0:T(8,128)}, f32[2,256,256]{2,1,0...) custom-call(s32[8,2]{1,0:T(8,128)} %copy.9.offsets, s32[1]{0:T(128)S(6)} %copy.11.live, f32[2,512,256]{2,1,0:T(8,128)} %own.1, ...), custom_call_target="tpu_custom_call" | custom-call | tf_op jit(solution)/shard_map/slots/pallas_call | solution.py:247
  41.1 8.1 %collective-permute-start.4 = (f32[2,256,256]{2,1,0:T(8,128)}, f32[2,256,256]{2,1,0:T(8,128)S(1)}, u32[]{:S(2)}, u32[]{:S(2)}) collective-permute-start(f32[2,256,256]{2,1,0:T(8,128)} %get-tuple-element.61), channel_id=1, source_target_pairs={{0,1},{1,2},{2,3},{4,5},{5,6},{6,7},{8,9},{9,10},{10,11},{12,13},{... | collective-permute-start | bytes 1572872 | tf_op jit(solution)/shard_map/ppermute | solution.py:278
  49.2 1.7 %collective-permute-done.4 = f32[2,256,256]{2,1,0:T(8,128)S(1)} collective-permute-done((f32[2,256,256]{2,1,0:T(8,128)}, f32[2,256,256]{2,1,0:T(8,128)S(1)}, u32[]{:S(2)}, u32[]{:S(2)}) %collective-permute-start.4) | collective-permute-done | bytes 524320 | tf_op jit(solution)/shard_map/ppermute | solution.py:278
  50.9 1.1 add.19
  52.1 10.3 %collective-permute-start.5 = (f32[1024,256]{1,0:T(8,128)}, f32[1024,256]{1,0:T(8,128)S(1)}, u32[]{:S(2)}, u32[]{:S(2)}) collective-permute-start(f32[1024,256]{1,0:T(8,128)} %get-tuple-element.65), channel_id=1, source_target_pairs={{0,1},{1,0},{2,3},{3,2},{4,5},{5,4},{6,7},{7,6},{8,9},{9,8},{10,11... | collective-permute-start | bytes 3145736 | tf_op jit(solution)/shard_map/ppermute | solution.py:295
  62.4 2.1 %collective-permute-start.9 = (f32[2,256,256]{2,1,0:T(8,128)}, f32[2,256,256]{2,1,0:T(8,128)S(1)}, u32[]{:S(2)}, u32[]{:S(2)}) collective-permute-start(f32[2,256,256]{2,1,0:T(8,128)} %get-tuple-element.70), channel_id=1, source_target_pairs={{0,1},{1,2},{2,3},{4,5},{5,6},{6,7},{8,9},{9,10},{10,11},{12,13},{... | collective-permute-start | bytes 1572872 | tf_op jit(solution)/shard_map/ppermute | solution.py:278
  64.5 1.3 collective-permute-start.11
  65.8 16.2 %collective-permute-start.10 = (f32[2,256,256]{2,1,0:T(8,128)S(1)}, f32[2,256,256]{2,1,0:T(8,128)S(1)}, u32[]{:S(2)}, u32[]{:S(2)}) collective-permute-start(f32[2,256,256]{2,1,0:T(8,128)S(1)} %add.19), channel_id=1, source_target_pairs={{0,4},{4,8},{8,12},{12,16},{16,20},{20,24},{24,28},{1,5},{5,9},{9,... | collective-permute-start | bytes 1572872 | tf_op jit(solution)/shard_map/ppermute | solution.py:278
  82.2 2.7 %collective-permute-start.6 = (f32[256,256]{1,0:T(8,128)S(1)}, f32[256,256]{1,0:T(8,128)S(1)}, u32[]{:S(2)}, u32[]{:S(2)}) collective-permute-start(f32[256,256]{1,0:T(8,128)S(1)} %get-tuple-element.67), channel_id=1, source_target_pairs={{0,2},{1,3},{2,0},{3,1},{4,6},{5,7},{6,4},{7,5},{8,10},{9,11},{10,... | collective-permute-start | bytes 786440 | tf_op jit(solution)/shard_map/ppermute | solution.py:295
  84.9 1.5 %collective-permute-start.8 = (f32[256,256]{1,0:T(8,128)S(1)}, f32[256,256]{1,0:T(8,128)S(1)}, u32[]{:S(2)}, u32[]{:S(2)}) collective-permute-start(f32[256,256]{1,0:T(8,128)S(1)} %get-tuple-element.69), channel_id=1, source_target_pairs={{0,6},{1,7},{2,4},{3,5},{4,2},{5,3},{6,0},{7,1},{8,14},{9,15},{10,... | collective-permute-start | bytes 786440 | tf_op jit(solution)/shard_map/ppermute | solution.py:295
  86.4 6.8 %collective-permute-done.10 = f32[2,256,256]{2,1,0:T(8,128)S(1)} collective-permute-done((f32[2,256,256]{2,1,0:T(8,128)S(1)}, f32[2,256,256]{2,1,0:T(8,128)S(1)}, u32[]{:S(2)}, u32[]{:S(2)}) %collective-permute-start.10) | collective-permute-done | bytes 524320 | tf_op jit(solution)/shard_map/ppermute | solution.py:278
  93.2 5.6 %collective-permute-done.7.refs_2_ = f32[256,256]{1,0:T(8,128)S(1)} collective-permute-done((f32[256,256]{1,0:T(8,128)S(1)}, f32[256,256]{1,0:T(8,128)S(1)}, u32[]{:S(2)}, u32[]{:S(2)}) %collective-permute-start.7) | collective-permute-done | bytes 262176 | tf_op jit(solution)/shard_map/ppermute | solution.py:295
  98.8 5.6 %collective-permute-done.8.refs_3_ = f32[256,256]{1,0:T(8,128)S(1)} collective-permute-done((f32[256,256]{1,0:T(8,128)S(1)}, f32[256,256]{1,0:T(8,128)S(1)}, u32[]{:S(2)}, u32[]{:S(2)}) %collective-permute-start.8) | collective-permute-done | bytes 262176 | tf_op jit(solution)/shard_map/ppermute | solution.py:295
  104.5 13.0 %collective-permute-start.12 = (f32[64,256]{1,0:T(8,128)S(1)}, f32[64,256]{1,0:T(8,128)S(1)}, u32[]{:S(2)}, u32[]{:S(2)}) collective-permute-start(f32[64,256]{1,0:T(8,128)S(1)} %get-tuple-element.81), channel_id=1, source_target_pairs={{0,8},{1,9},{2,10},{3,11},{4,12},{5,13},{6,14},{7,15},{8,0},{9,1},... | collective-permute-start | bytes 196616 | tf_op jit(solution)/shard_map/ppermute | solution.py:295
  117.5 2.4 %collective-permute-start.14 = (f32[64,256]{1,0:T(8,128)S(1)}, f32[64,256]{1,0:T(8,128)S(1)}, u32[]{:S(2)}, u32[]{:S(2)}) collective-permute-start(f32[64,256]{1,0:T(8,128)S(1)} %get-tuple-element.83), channel_id=1, source_target_pairs={{0,24},{1,25},{2,26},{3,27},{4,28},{5,29},{6,30},{7,31},{8,16},{9,... | collective-permute-start | bytes 196616 | tf_op jit(solution)/shard_map/ppermute | solution.py:295
  120.0 5.0 %collective-permute-done.13.refs_2_ = f32[64,256]{1,0:T(8,128)S(1)} collective-permute-done((f32[64,256]{1,0:T(8,128)S(1)}, f32[64,256]{1,0:T(8,128)S(1)}, u32[]{:S(2)}, u32[]{:S(2)}) %collective-permute-start.13) | collective-permute-done | bytes 65568 | tf_op jit(solution)/shard_map/ppermute | solution.py:295
  125.0 1.4 collective-permute-start.17
  126.4 1.9 %collective-permute-start.16 = (f32[64,256]{1,0:T(8,128)S(1)}, f32[64,256]{1,0:T(8,128)S(1)}, u32[]{:S(2)}, u32[]{:S(2)}) collective-permute-start(f32[64,256]{1,0:T(8,128)S(1)} %add_parts.5.refs_0_), channel_id=1, source_target_pairs={{0,16},{1,17},{2,18},{3,19},{4,20},{5,21},{6,22},{7,23},{8,24},{9,... | collective-permute-start | bytes 196616 | tf_op jit(solution)/shard_map/ppermute | solution.py:295
  129.5 2.4 %collective-permute-done.17.refs_3_ = f32[64,256]{1,0:T(8,128)S(1)} collective-permute-done((f32[64,256]{1,0:T(8,128)S(1)}, f32[64,256]{1,0:T(8,128)S(1)}, u32[]{:S(2)}, u32[]{:S(2)}) %collective-permute-start.17) | collective-permute-done | bytes 65568 | tf_op jit(solution)/shard_map/ppermute | solution.py:295
  131.9 2.6 %collective-permute-done.16.refs_2_ = f32[64,256]{1,0:T(8,128)S(1)} collective-permute-done((f32[64,256]{1,0:T(8,128)S(1)}, f32[64,256]{1,0:T(8,128)S(1)}, u32[]{:S(2)}, u32[]{:S(2)}) %collective-permute-start.16) | collective-permute-done | bytes 65568 | tf_op jit(solution)/shard_map/ppermute | solution.py:295
  134.7 2.3 %collective-permute-start.19 = (f32[256,256]{1,0:T(8,128)S(1)}, f32[256,256]{1,0:T(8,128)S(1)}, u32[]{:S(2)}, u32[]{:S(2)}) collective-permute-start(f32[256,256]{1,0:T(8,128)S(1)} %join_parts.2.refs_0_), channel_id=1, source_target_pairs={{0,4},{1,5},{2,6},{3,7},{4,0},{5,1},{6,2},{7,3},{8,12},{9,13},{10,... | collective-permute-start | bytes 786440 | tf_op jit(solution)/shard_map/ppermute | solution.py:295
  137.0 1.2 collective-permute-start.18
  138.4 6.5 %collective-permute-done.20.refs_3_ = f32[256,256]{1,0:T(8,128)S(1)} collective-permute-done((f32[256,256]{1,0:T(8,128)S(1)}, f32[256,256]{1,0:T(8,128)S(1)}, u32[]{:S(2)}, u32[]{:S(2)}) %collective-permute-start.20) | collective-permute-done | bytes 262176 | tf_op jit(solution)/shard_map/ppermute | solution.py:295
  144.8 3.6 %collective-permute-done.19.refs_2_ = f32[256,256]{1,0:T(8,128)S(1)} collective-permute-done((f32[256,256]{1,0:T(8,128)S(1)}, f32[256,256]{1,0:T(8,128)S(1)}, u32[]{:S(2)}, u32[]{:S(2)}) %collective-permute-start.19) | collective-permute-done | bytes 262176 | tf_op jit(solution)/shard_map/ppermute | solution.py:295
  150.5 1.5 join_parts.3
  (43 shorter events, 6.2 us)
Async XLA Ops:
  0.6 20.8 %copy-start.6 = (s32[8,2]{0,1:T(2,128)S(1)}, s32[8,2]{0,1:T(2,128)}, u32[]{:S(2)}) copy-start(s32[8,2]{0,1:T(2,128)} %param.16) | copy-start | bytes 196
  1.9 17.6 %collective-permute-start.1 = (f32[2,256,256]{2,1,0:T(8,128)S(1)}, f32[2,256,256]{2,1,0:T(8,128)S(1)}, u32[]{:S(2)}, u32[]{:S(2)}) collective-permute-start(f32[2,256,256]{2,1,0:T(8,128)S(1)} %get-tuple-element.85), channel_id=1, source_target_pairs={{4,0},{8,4},{12,8},{16,12},{20,16},{24,20},{28,24},{5,1},{9,5},{13... | collective-permute-start | bytes 1572872 | tf_op jit(solution)/shard_map/ppermute | solution.py:278
  3.2 26.7 %collective-permute-start = (f32[2,256,256]{2,1,0:T(8,128)S(1)}, f32[2,256,256]{2,1,0:T(8,128)S(1)}, u32[]{:S(2)}, u32[]{:S(2)}) collective-permute-start(f32[2,256,256]{2,1,0:T(8,128)S(1)} %get-tuple-element.85), channel_id=1, source_target_pairs={{1,0},{2,1},{3,2},{5,4},{6,5},{7,6},{9,8},{10,9},{11,10},{13,12},{... | collective-permute-start | bytes 1572872 | tf_op jit(solution)/shard_map/ppermute | solution.py:278
  4.5 25.4 %collective-permute-start.2 = (f32[2,256,256]{2,1,0:T(8,128)S(1)}, f32[2,256,256]{2,1,0:T(8,128)S(1)}, u32[]{:S(2)}, u32[]{:S(2)}) collective-permute-start(f32[2,256,256]{2,1,0:T(8,128)S(1)} %get-tuple-element.84), channel_id=1, source_target_pairs={{4,0},{8,4},{12,8},{16,12},{20,16},{24,20},{28,24},{5,1},{9,5},{13... | collective-permute-start | bytes 1572872 | tf_op jit(solution)/shard_map/ppermute | solution.py:278
  19.5 10.4 %copy-start.2 = (f32[2,256,256]{2,1,0:T(8,128)}, f32[2,256,256]{2,1,0:T(8,128)S(1)}, u32[]{:S(2)}) copy-start(f32[2,256,256]{2,1,0:T(8,128)S(1)} %collective-permute-done.1.right) | copy-start | bytes 1572868
  19.5 10.4 %collective-permute-start.3 = (f32[2,256,256]{2,1,0:T(8,128)S(1)}, f32[2,256,256]{2,1,0:T(8,128)S(1)}, u32[]{:S(2)}, u32[]{:S(2)}) collective-permute-start(f32[2,256,256]{2,1,0:T(8,128)S(1)} %collective-permute-done.1.right), channel_id=1, source_target_pairs={{1,0},{2,1},{3,2},{5,4},{6,5},{7,6},{9,8},{10,9},{11,10},{13,12},{... | collective-permute-start | bytes 1572872 | tf_op jit(solution)/shard_map/ppermute | solution.py:278
  29.9 0.8 copy-start.4
  29.9 1.0 copy-start.3
  30.9 0.8 copy-start.5
  41.1 41.0 %copy-start = (f32[1024,256]{1,0:T(8,128)S(1)}, f32[1024,256]{1,0:T(8,128)}, u32[]{:S(2)}) copy-start(f32[1024,256]{1,0:T(8,128)} %get-tuple-element.64.refs_0_) | copy-start | bytes 3145732
  41.1 9.8 %collective-permute-start.4 = (f32[2,256,256]{2,1,0:T(8,128)}, f32[2,256,256]{2,1,0:T(8,128)S(1)}, u32[]{:S(2)}, u32[]{:S(2)}) collective-permute-start(f32[2,256,256]{2,1,0:T(8,128)} %get-tuple-element.61), channel_id=1, source_target_pairs={{0,1},{1,2},{2,3},{4,5},{5,6},{6,7},{8,9},{9,10},{10,11},{12,13},{... | collective-permute-start | bytes 1572872 | tf_op jit(solution)/shard_map/ppermute | solution.py:278
  52.1 86.1 %copy-start.1 = (f32[2,512,256]{2,1,0:T(8,128)S(1)}, f32[2,512,256]{2,1,0:T(8,128)}, u32[]{:S(2)}) copy-start(f32[2,512,256]{2,1,0:T(8,128)} %get-tuple-element.59) | copy-start | bytes 3145732
  52.1 30.0 %collective-permute-start.5 = (f32[1024,256]{1,0:T(8,128)}, f32[1024,256]{1,0:T(8,128)S(1)}, u32[]{:S(2)}, u32[]{:S(2)}) collective-permute-start(f32[1024,256]{1,0:T(8,128)} %get-tuple-element.65), channel_id=1, source_target_pairs={{0,1},{1,0},{2,3},{3,2},{4,5},{5,4},{6,7},{7,6},{8,9},{9,8},{10,11... | collective-permute-start | bytes 3145736 | tf_op jit(solution)/shard_map/ppermute | solution.py:295
  62.4 22.5 %collective-permute-start.9 = (f32[2,256,256]{2,1,0:T(8,128)}, f32[2,256,256]{2,1,0:T(8,128)S(1)}, u32[]{:S(2)}, u32[]{:S(2)}) collective-permute-start(f32[2,256,256]{2,1,0:T(8,128)} %get-tuple-element.70), channel_id=1, source_target_pairs={{0,1},{1,2},{2,3},{4,5},{5,6},{6,7},{8,9},{9,10},{10,11},{12,13},{... | collective-permute-start | bytes 1572872 | tf_op jit(solution)/shard_map/ppermute | solution.py:278
  64.5 21.9 %collective-permute-start.11 = (f32[2,256,256]{2,1,0:T(8,128)}, f32[2,256,256]{2,1,0:T(8,128)S(1)}, u32[]{:S(2)}, u32[]{:S(2)}) collective-permute-start(f32[2,256,256]{2,1,0:T(8,128)} %get-tuple-element.72), channel_id=1, source_target_pairs={{0,4},{4,8},{8,12},{12,16},{16,20},{20,24},{24,28},{1,5},{5,9},{9,... | collective-permute-start | bytes 1572872 | tf_op jit(solution)/shard_map/ppermute | solution.py:278
  65.8 27.4 %collective-permute-start.10 = (f32[2,256,256]{2,1,0:T(8,128)S(1)}, f32[2,256,256]{2,1,0:T(8,128)S(1)}, u32[]{:S(2)}, u32[]{:S(2)}) collective-permute-start(f32[2,256,256]{2,1,0:T(8,128)S(1)} %add.19), channel_id=1, source_target_pairs={{0,4},{4,8},{8,12},{12,16},{16,20},{20,24},{24,28},{1,5},{5,9},{9,... | collective-permute-start | bytes 1572872 | tf_op jit(solution)/shard_map/ppermute | solution.py:278
  82.2 11.0 %collective-permute-start.6 = (f32[256,256]{1,0:T(8,128)S(1)}, f32[256,256]{1,0:T(8,128)S(1)}, u32[]{:S(2)}, u32[]{:S(2)}) collective-permute-start(f32[256,256]{1,0:T(8,128)S(1)} %get-tuple-element.67), channel_id=1, source_target_pairs={{0,2},{1,3},{2,0},{3,1},{4,6},{5,7},{6,4},{7,5},{8,10},{9,11},{10,... | collective-permute-start | bytes 786440 | tf_op jit(solution)/shard_map/ppermute | solution.py:295
  84.9 13.9 %collective-permute-start.7 = (f32[256,256]{1,0:T(8,128)S(1)}, f32[256,256]{1,0:T(8,128)S(1)}, u32[]{:S(2)}, u32[]{:S(2)}) collective-permute-start(f32[256,256]{1,0:T(8,128)S(1)} %get-tuple-element.68), channel_id=1, source_target_pairs={{0,4},{1,5},{2,6},{3,7},{4,0},{5,1},{6,2},{7,3},{8,12},{9,13},{10,... | collective-permute-start | bytes 786440 | tf_op jit(solution)/shard_map/ppermute | solution.py:295
  84.9 19.6 %collective-permute-start.8 = (f32[256,256]{1,0:T(8,128)S(1)}, f32[256,256]{1,0:T(8,128)S(1)}, u32[]{:S(2)}, u32[]{:S(2)}) collective-permute-start(f32[256,256]{1,0:T(8,128)S(1)} %get-tuple-element.69), channel_id=1, source_target_pairs={{0,6},{1,7},{2,4},{3,5},{4,2},{5,3},{6,0},{7,1},{8,14},{9,15},{10,... | collective-permute-start | bytes 786440 | tf_op jit(solution)/shard_map/ppermute | solution.py:295
  104.5 15.5 %collective-permute-start.12 = (f32[64,256]{1,0:T(8,128)S(1)}, f32[64,256]{1,0:T(8,128)S(1)}, u32[]{:S(2)}, u32[]{:S(2)}) collective-permute-start(f32[64,256]{1,0:T(8,128)S(1)} %get-tuple-element.81), channel_id=1, source_target_pairs={{0,8},{1,9},{2,10},{3,11},{4,12},{5,13},{6,14},{7,15},{8,0},{9,1},... | collective-permute-start | bytes 196616 | tf_op jit(solution)/shard_map/ppermute | solution.py:295
  117.5 7.5 %collective-permute-start.13 = (f32[64,256]{1,0:T(8,128)S(1)}, f32[64,256]{1,0:T(8,128)S(1)}, u32[]{:S(2)}, u32[]{:S(2)}) collective-permute-start(f32[64,256]{1,0:T(8,128)S(1)} %get-tuple-element.82), channel_id=1, source_target_pairs={{0,16},{1,17},{2,18},{3,19},{4,20},{5,21},{6,22},{7,23},{8,24},{9,... | collective-permute-start | bytes 196616 | tf_op jit(solution)/shard_map/ppermute | solution.py:295
  117.5 7.5 %collective-permute-start.14 = (f32[64,256]{1,0:T(8,128)S(1)}, f32[64,256]{1,0:T(8,128)S(1)}, u32[]{:S(2)}, u32[]{:S(2)}) collective-permute-start(f32[64,256]{1,0:T(8,128)S(1)} %get-tuple-element.83), channel_id=1, source_target_pairs={{0,24},{1,25},{2,26},{3,27},{4,28},{5,29},{6,30},{7,31},{8,16},{9,... | collective-permute-start | bytes 196616 | tf_op jit(solution)/shard_map/ppermute | solution.py:295
  125.0 6.9 %collective-permute-start.17 = (f32[64,256]{1,0:T(8,128)S(1)}, f32[64,256]{1,0:T(8,128)S(1)}, u32[]{:S(2)}, u32[]{:S(2)}) collective-permute-start(f32[64,256]{1,0:T(8,128)S(1)} %add_parts.5.refs_0_), channel_id=1, source_target_pairs={{0,24},{1,25},{2,26},{3,27},{4,28},{5,29},{6,30},{7,31},{8,16},{9,... | collective-permute-start | bytes 196616 | tf_op jit(solution)/shard_map/ppermute | solution.py:295
  126.4 8.1 %collective-permute-start.16 = (f32[64,256]{1,0:T(8,128)S(1)}, f32[64,256]{1,0:T(8,128)S(1)}, u32[]{:S(2)}, u32[]{:S(2)}) collective-permute-start(f32[64,256]{1,0:T(8,128)S(1)} %add_parts.5.refs_0_), channel_id=1, source_target_pairs={{0,16},{1,17},{2,18},{3,19},{4,20},{5,21},{6,22},{7,23},{8,24},{9,... | collective-permute-start | bytes 196616 | tf_op jit(solution)/shard_map/ppermute | solution.py:295
  128.4 6.1 %collective-permute-start.15 = (f32[64,256]{1,0:T(8,128)S(1)}, f32[64,256]{1,0:T(8,128)S(1)}, u32[]{:S(2)}, u32[]{:S(2)}) collective-permute-start(f32[64,256]{1,0:T(8,128)S(1)} %add_parts.5.refs_0_), channel_id=1, source_target_pairs={{0,8},{1,9},{2,10},{3,11},{4,12},{5,13},{6,14},{7,15},{8,0},{9,1},... | collective-permute-start | bytes 196616 | tf_op jit(solution)/shard_map/ppermute | solution.py:295
  134.6 10.2 %collective-permute-start.20 = (f32[256,256]{1,0:T(8,128)S(1)}, f32[256,256]{1,0:T(8,128)S(1)}, u32[]{:S(2)}, u32[]{:S(2)}) collective-permute-start(f32[256,256]{1,0:T(8,128)S(1)} %join_parts.2.refs_0_), channel_id=1, source_target_pairs={{0,6},{1,7},{2,4},{3,5},{4,2},{5,3},{6,0},{7,1},{8,14},{9,15},{10,... | collective-permute-start | bytes 786440 | tf_op jit(solution)/shard_map/ppermute | solution.py:295
  134.7 13.8 %collective-permute-start.19 = (f32[256,256]{1,0:T(8,128)S(1)}, f32[256,256]{1,0:T(8,128)S(1)}, u32[]{:S(2)}, u32[]{:S(2)}) collective-permute-start(f32[256,256]{1,0:T(8,128)S(1)} %join_parts.2.refs_0_), channel_id=1, source_target_pairs={{0,4},{1,5},{2,6},{3,7},{4,0},{5,1},{6,2},{7,3},{8,12},{9,13},{10,... | collective-permute-start | bytes 786440 | tf_op jit(solution)/shard_map/ppermute | solution.py:295
  137.0 12.0 %collective-permute-start.18 = (f32[256,256]{1,0:T(8,128)S(1)}, f32[256,256]{1,0:T(8,128)S(1)}, u32[]{:S(2)}, u32[]{:S(2)}) collective-permute-start(f32[256,256]{1,0:T(8,128)S(1)} %join_parts.2.refs_0_), channel_id=1, source_target_pairs={{0,2},{1,3},{2,0},{3,1},{4,6},{5,7},{6,4},{7,5},{8,10},{9,11},{10,... | collective-permute-start | bytes 786440 | tf_op jit(solution)/shard_map/ppermute | solution.py:295
  138.3 11.8 %collective-permute-start.21 = (f32[256,256]{1,0:T(8,128)S(1)}, f32[256,256]{1,0:T(8,128)S(1)}, u32[]{:S(2)}, u32[]{:S(2)}) collective-permute-start(f32[256,256]{1,0:T(8,128)S(1)} %join_parts.2.refs_0_), channel_id=1, source_target_pairs={{0,1},{1,0},{2,3},{3,2},{4,5},{5,4},{6,7},{7,6},{8,9},{9,8},{10,11... | collective-permute-start | bytes 786440 | tf_op jit(solution)/shard_map/ppermute | solution.py:295
  144.8 5.3 %collective-permute-start.24 = (f32[256,256]{1,0:T(8,128)S(1)}, f32[256,256]{1,0:T(8,128)S(1)}, u32[]{:S(2)}, u32[]{:S(2)}) collective-permute-start(f32[256,256]{1,0:T(8,128)S(1)} %collective-permute-done.20.refs_3_), channel_id=1, source_target_pairs={{0,1},{1,0},{2,3},{3,2},{4,5},{5,4},{6,7},{7,6},{8,9},{9,8},{10,11... | collective-permute-start | bytes 786440 | tf_op jit(solution)/shard_map/ppermute | solution.py:295
  148.4 1.7 %collective-permute-start.23 = (f32[256,256]{1,0:T(8,128)S(1)}, f32[256,256]{1,0:T(8,128)S(1)}, u32[]{:S(2)}, u32[]{:S(2)}) collective-permute-start(f32[256,256]{1,0:T(8,128)S(1)} %collective-permute-done.19.refs_2_), channel_id=1, source_target_pairs={{0,1},{1,0},{2,3},{3,2},{4,5},{5,4},{6,7},{7,6},{8,9},{9,8},{10,11... | collective-permute-start | bytes 786440 | tf_op jit(solution)/shard_map/ppermute | solution.py:295
  149.0 1.5 %collective-permute-start.22 = (f32[256,256]{1,0:T(8,128)S(1)}, f32[256,256]{1,0:T(8,128)S(1)}, u32[]{:S(2)}, u32[]{:S(2)}) collective-permute-start(f32[256,256]{1,0:T(8,128)S(1)} %collective-permute-done.18.refs_1_), channel_id=1, source_target_pairs={{0,1},{1,0},{2,3},{3,2},{4,5},{5,4},{6,7},{7,6},{8,9},{9,8},{10,11... | collective-permute-start | bytes 786440 | tf_op jit(solution)/shard_map/ppermute | solution.py:295
where the time goes:
time: 153 us; the launch traced here: 152 us
  starting transfers between devices  71 us (46%)
  waiting for transfers between devices  62.3 us (41%)
  Pallas kernels  11.1 us (7%)
  local copies, waits for them, and re-layouts  3.74 us (2%)
  other arithmetic  2.34 us (2%)
    ppermute x17, starting transfers between devices, swapped(): lax.ppermute(value, ('wide', 'narrow'), [(source, source ^ mask) for sour...  38.1 us
    ppermute x8, starting transfers between devices, shifted(): lax.ppermute(value, axis, [(source, source + steps) for source in range(f...  32.9 us
    ppermute x17, waiting for transfers between devices, swapped(): lax.ppermute(value, ('wide', 'narrow'), [(source, source ^ mask) for sour...  32.4 us
    ppermute x8, waiting for transfers between devices, shifted(): lax.ppermute(value, axis, [(source, source + steps) for source in range(f...  30 us
    pallas_call x1, Pallas kernels, run_slots(): pl.pallas_call(functools.partial(slots_kernel, tile_rows, tile_cols), out...  9.37 us
  transfers between devices with their start and end apart: 25, of which 13 were waited for; matrix products, arithmetic and copies ran while one was open for 1% of the time, Pallas kernels for 0%

commit v1 on v0

--- a/solution.py
+++ b/solution.py
@@ -340,23 +340,39 @@
     )(*parts)
 
 
-def sum_everywhere(keep, send, scale, beside):
+def together(*values):
+    return lax.optimization_barrier(values)
+
+
+def sum_and_shift(keep, send, scale, grad_below, grad_right, grad_right_low, grad_corner):
     narrow, wide = lax.axis_size("narrow"), lax.axis_size("wide")
     bits = [1 << n for n in range((narrow * wide).bit_length() - 1)]
-    groups = [tuple(bits[n : n + 2]) for n in range(1, len(bits), 2)]
+    groups = [(bits[1],)] + [tuple(bits[n : n + 2]) for n in range(2, len(bits), 2)]
     parts = [keep, swapped(send, bits[0])]
-    for group in groups:
+    came_right_low = shifted(grad_right_low, "wide", 1)
+    for n, group in enumerate(groups):
         pieces = add_parts(parts, group)
+        if n == 1:
+            pieces, grad_corner = together(pieces, grad_corner)
+            came_corner = shifted(grad_corner, "narrow", 1)
+        if n == 2:
+            pieces, grad_below = together(pieces, grad_below)
+            came_below = shifted(grad_below, "narrow", 1)
         parts = [pieces[0]] + [swapped(piece, mask) for piece, mask in zip(pieces[1:], partners(group)[1:])]
-        if group == groups[0]:
-            parts, beside = lax.optimization_barrier((parts, beside))
+        if n == 0:
+            parts, came_right_low = together(parts, came_right_low)
     value = add_parts(parts, ())[0]
     for group in reversed(groups):
+        if group == groups[0]:
+            value, grad_right = together(value, grad_right + came_corner)
+            came_right = shifted(grad_right, "wide", 1)
         parts = [value] + [swapped(value, mask) for mask in partners(group)[1:]]
+        if group == groups[-1]:
+            parts, came_below = together(parts, came_below)
         if group != groups[0]:
             value = join_parts(parts, group)
     parts = parts + [swapped(part, bits[0]) for part in parts]
-    return join_parts(parts, groups[0] + (bits[0],), scale), beside
+    return join_parts(parts, groups[0] + (bits[0],), scale), came_below, came_right, came_right_low
 
 
 def on_device(object_field, probe, amplitudes, offsets, live):
@@ -369,11 +385,10 @@
     grad_own, grad_below, grad_right, grad_right_low, grad_corner, keep, send = run_slots(
         offsets, live, object_field, below, right, right_low, corner, probe, amplitudes
     )
-    grad_right, keep, send = lax.optimization_barrier((grad_right + shifted(grad_corner, "narrow", 1), keep, send))
-    beside = [shifted(grad_below, "narrow", 1), shifted(grad_right, "wide", 1), shifted(grad_right_low, "wide", 1)]
     total_slots = lax.axis_size("wide") * lax.axis_size("narrow") * offsets.shape[0]
-    probe_grad, beside = sum_everywhere(keep, send, 1.0 / math.sqrt(total_slots), beside)
-    came_below, came_right, came_right_low = beside
+    probe_grad, came_below, came_right, came_right_low = sum_and_shift(
+        keep, send, 1.0 / math.sqrt(total_slots), grad_below, grad_right, grad_right_low, grad_corner
+    )
     rims = jnp.concatenate([came_right, came_right_low], 1)
     object_grad = grad_own.at[:, :extent, :].add(came_below).at[:, :, :extent].add(rims)
     return (object_grad, probe_grad.reshape(probe.shape))

time: 153 us -> 133 us (0.87); the launches traced: 152 us -> 134 us
  starting transfers between devices: 71 us -> 48 us
  waiting for transfers between devices: 62.3 us -> 67.3 us
    ppermute x8, starting transfers between devices: 32.9 us -> 17.4 us  [shifted(): lax.ppermute(value, axis, [(source, source + steps) for source in range(f...]
    ppermute x17 -> x13, waiting for transfers between devices: 32.4 us -> 45.8 us  [swapped(): lax.ppermute(value, ('wide', 'narrow'), [(source, source ^ mask) for sour...]
    ppermute x8, waiting for transfers between devices: 30 us -> 21.5 us  [shifted(): lax.ppermute(value, axis, [(source, source + steps) for source in range(f...]
    ppermute x17 -> x13, starting transfers between devices: 38.1 us -> 30.6 us  [swapped(): lax.ppermute(value, ('wide', 'narrow'), [(source, source ^ mask) for sour...]
    unnamed x15 -> x21, local copies, waits for them, and re-layouts: 2.45 us -> 3.68 us
  transfers between devices with their start and end apart: 25 -> 21, of which waited for: 13 -> 13; matrix products, arithmetic and copies ran while one was open for 1% -> 1% of each run, Pallas kernels for 0% -> 0%
where the time goes in v1:
time: 133 us; the launch traced here: 134 us
  waiting for transfers between devices  67.3 us (51%)
  starting transfers between devices  48 us (36%)
  Pallas kernels  11.1 us (8%)
  local copies, waits for them, and re-layouts  4.96 us (4%)
  between operations  1.54 us (1%)
    ppermute x13, waiting for transfers between devices, swapped(): lax.ppermute(value, ('wide', 'narrow'), [(source, source ^ mask) for sour...  45.8 us
    ppermute x13, starting transfers between devices, swapped(): lax.ppermute(value, ('wide', 'narrow'), [(source, source ^ mask) for sour...  30.6 us
    ppermute x8, waiting for transfers between devices, shifted(): lax.ppermute(value, axis, [(source, source + steps) for source in range(f...  21.5 us
    ppermute x8, starting transfers between devices, shifted(): lax.ppermute(value, axis, [(source, source + steps) for source in range(f...  17.4 us
    pallas_call x1, Pallas kernels, run_slots(): pl.pallas_call(functools.partial(slots_kernel, tile_rows, tile_cols), out...  9.37 us
    unnamed x21, local copies, waits for them, and re-layouts  3.68 us
  transfers between devices with their start and end apart: 21, of which 13 were waited for; matrix products, arithmetic and copies ran while one was open for 1% of the time, Pallas kernels for 0%

profile of v1, /device:TPU:0, one launch (start us, length us, event | category | flops | bytes accessed | tf_op | source)
XLA Modules:
  0.0 134.2 jit_solution(9466493306507252946)
XLA Ops:
  0.6 1.3 fusion
  1.9 1.3 collective-permute-start.1
  3.2 1.3 collective-permute-start
  4.5 1.3 collective-permute-start.2
  5.8 13.7 %collective-permute-done.1.right = f32[2,256,256]{2,1,0:T(8,128)S(1)} collective-permute-done((f32[2,256,256]{2,1,0:T(8,128)S(1)}, f32[2,256,256]{2,1,0:T(8,128)S(1)}, u32[]{:S(2)}, u32[]{:S(2)}) %collective-permute-start.1) | collective-permute-done | bytes 524320 | tf_op jit(solution)/shard_map/ppermute | solution.py:278
  19.5 1.3 collective-permute-start.3
  21.5 0.7 copy.9.offsets
  22.1 7.8 %collective-permute-done.2.right_low = f32[2,256,256]{2,1,0:T(8,128)S(1)} collective-permute-done((f32[2,256,256]{2,1,0:T(8,128)S(1)}, f32[2,256,256]{2,1,0:T(8,128)S(1)}, u32[]{:S(2)}, u32[]{:S(2)}) %collective-permute-start.2) | collective-permute-done | bytes 524320 | tf_op jit(solution)/shard_map/ppermute | solution.py:278
  30.0 0.8 copy-done.5
  30.9 0.8 copy-done.6
  31.7 9.4 %slots.1 = (f32[2,512,256]{2,1,0:T(8,128)}, f32[2,256,256]{2,1,0:T(8,128)}, f32[2,256,256]{2,1,0:T(8,128)}, f32[2,256,256]{2,1,0:T(8,128)}, f32[2,256,256]{2,1,0...) custom-call(s32[8,2]{1,0:T(8,128)} %copy.9.offsets, s32[1]{0:T(128)S(6)} %copy.11.live, f32[2,512,256]{2,1,0:T(8,128)} %own.1, ...), custom_call_target="tpu_custom_call" | custom-call | tf_op jit(solution)/shard_map/slots/pallas_call | solution.py:247
  41.1 6.1 %collective-permute-start.4 = (f32[1024,256]{1,0:T(8,128)}, f32[1024,256]{1,0:T(8,128)S(1)}, u32[]{:S(2)}, u32[]{:S(2)}) collective-permute-start(f32[1024,256]{1,0:T(8,128)} %get-tuple-element.67), channel_id=1, source_target_pairs={{0,1},{1,0},{2,3},{3,2},{4,5},{5,4},{6,7},{7,6},{8,9},{9,8},{10,11... | collective-permute-start | bytes 3145736 | tf_op jit(solution)/shard_map/ppermute | solution.py:295
  47.2 4.3 %collective-permute-start.6 = (f32[2,256,256]{2,1,0:T(8,128)}, f32[2,256,256]{2,1,0:T(8,128)S(1)}, u32[]{:S(2)}, u32[]{:S(2)}) collective-permute-start(f32[2,256,256]{2,1,0:T(8,128)} %get-tuple-element.70), channel_id=1, source_target_pairs={{0,4},{4,8},{8,12},{12,16},{16,20},{20,24},{24,28},{1,5},{5,9},{9,... | collective-permute-start | bytes 1572872 | tf_op jit(solution)/shard_map/ppermute | solution.py:278
  51.6 1.2 copy-done
  52.9 17.1 %collective-permute-start.5 = (f32[512,256]{1,0:T(8,128)S(1)}, f32[512,256]{1,0:T(8,128)S(1)}, u32[]{:S(2)}, u32[]{:S(2)}) collective-permute-start(f32[512,256]{1,0:T(8,128)S(1)} %get-tuple-element.69), channel_id=1, source_target_pairs={{0,2},{1,3},{2,0},{3,1},{4,6},{5,7},{6,4},{7,5},{8,10},{9,11},{10,... | collective-permute-start | bytes 1572872 | tf_op jit(solution)/shard_map/ppermute | solution.py:295
  70.0 12.2 %collective-permute-done.5.refs_1_ = f32[512,256]{1,0:T(8,128)S(1)} collective-permute-done((f32[512,256]{1,0:T(8,128)S(1)}, f32[512,256]{1,0:T(8,128)S(1)}, u32[]{:S(2)}, u32[]{:S(2)}) %collective-permute-start.5) | collective-permute-done | bytes 524320 | tf_op jit(solution)/shard_map/ppermute | solution.py:295
  82.5 3.4 %collective-permute-start.9 = (f32[128,256]{1,0:T(8,128)S(1)}, f32[128,256]{1,0:T(8,128)S(1)}, u32[]{:S(2)}, u32[]{:S(2)}) collective-permute-start(f32[128,256]{1,0:T(8,128)S(1)} %get-tuple-element.81), channel_id=1, source_target_pairs={{0,12},{1,13},{2,14},{3,15},{4,8},{5,9},{6,10},{7,11},{8,4},{9,5},... | collective-permute-start | bytes 393224 | tf_op jit(solution)/shard_map/ppermute | solution.py:295
  85.9 2.0 %collective-permute-done.7.refs_1_ = f32[128,256]{1,0:T(8,128)S(1)} collective-permute-done((f32[128,256]{1,0:T(8,128)S(1)}, f32[128,256]{1,0:T(8,128)S(1)}, u32[]{:S(2)}, u32[]{:S(2)}) %collective-permute-start.7) | collective-permute-done | bytes 131104 | tf_op jit(solution)/shard_map/ppermute | solution.py:295
  87.9 1.0 collective-permute-done.8.refs_2_
  88.9 2.5 %collective-permute-done.9.refs_3_ = f32[128,256]{1,0:T(8,128)S(1)} collective-permute-done((f32[128,256]{1,0:T(8,128)S(1)}, f32[128,256]{1,0:T(8,128)S(1)}, u32[]{:S(2)}, u32[]{:S(2)}) %collective-permute-start.9) | collective-permute-done | bytes 131104 | tf_op jit(solution)/shard_map/ppermute | solution.py:295
  91.4 1.3 collective-permute-start.12
  92.8 4.1 %collective-permute-start.16 = (f32[2,256,256]{2,1,0:T(8,128)S(1)}, f32[2,256,256]{2,1,0:T(8,128)S(1)}, u32[]{:S(2)}, u32[]{:S(2)}) collective-permute-start(f32[2,256,256]{2,1,0:T(8,128)S(1)} %copy-done.8), channel_id=1, source_target_pairs={{0,1},{1,2},{2,3},{4,5},{5,6},{6,7},{8,9},{9,10},{10,11},{12,13},{... | collective-permute-start | bytes 1572872 | tf_op jit(solution)/shard_map/ppermute | solution.py:278
  96.9 6.0 %collective-permute-done.10.refs_1_ = f32[64,256]{1,0:T(8,128)S(1)} collective-permute-done((f32[64,256]{1,0:T(8,128)S(1)}, f32[64,256]{1,0:T(8,128)S(1)}, u32[]{:S(2)}, u32[]{:S(2)}) %collective-permute-start.10) | collective-permute-done | bytes 65568 | tf_op jit(solution)/shard_map/ppermute | solution.py:295
  103.0 5.4 %collective-permute-done.11.refs_1_ = f32[64,256]{1,0:T(8,128)S(1)} collective-permute-done((f32[64,256]{1,0:T(8,128)S(1)}, f32[64,256]{1,0:T(8,128)S(1)}, u32[]{:S(2)}, u32[]{:S(2)}) %collective-permute-start.11) | collective-permute-done | bytes 65568 | tf_op jit(solution)/shard_map/ppermute | solution.py:295
  108.5 2.0 %collective-permute-start.14 = (f32[128,256]{1,0:T(8,128)S(1)}, f32[128,256]{1,0:T(8,128)S(1)}, u32[]{:S(2)}, u32[]{:S(2)}) collective-permute-start(f32[128,256]{1,0:T(8,128)S(1)} %join_parts.3.refs_0_), channel_id=1, source_target_pairs={{0,8},{1,9},{2,10},{3,11},{4,12},{5,13},{6,14},{7,15},{8,0},{9,1},... | collective-permute-start | bytes 393224 | tf_op jit(solution)/shard_map/ppermute | solution.py:295
  110.5 1.5 %collective-permute-start.13 = (f32[128,256]{1,0:T(8,128)S(1)}, f32[128,256]{1,0:T(8,128)S(1)}, u32[]{:S(2)}, u32[]{:S(2)}) collective-permute-start(f32[128,256]{1,0:T(8,128)S(1)} %join_parts.3.refs_0_), channel_id=1, source_target_pairs={{0,4},{1,5},{2,6},{3,7},{4,0},{5,1},{6,2},{7,3},{8,12},{9,13},{10,... | collective-permute-start | bytes 393224 | tf_op jit(solution)/shard_map/ppermute | solution.py:295
  112.1 3.7 %collective-permute-done.15.refs_3_ = f32[128,256]{1,0:T(8,128)S(1)} collective-permute-done((f32[128,256]{1,0:T(8,128)S(1)}, f32[128,256]{1,0:T(8,128)S(1)}, u32[]{:S(2)}, u32[]{:S(2)}) %collective-permute-start.15) | collective-permute-done | bytes 131104 | tf_op jit(solution)/shard_map/ppermute | solution.py:295
  116.3 1.0 collective-permute-done.13.refs_1_
  117.4 2.5 %collective-permute-start.17 = (f32[2,256,256]{2,1,0:T(8,128)S(1)}, f32[2,256,256]{2,1,0:T(8,128)S(1)}, u32[]{:S(2)}, u32[]{:S(2)}) collective-permute-start(f32[2,256,256]{2,1,0:T(8,128)S(1)} %add.20), channel_id=1, source_target_pairs={{0,4},{4,8},{8,12},{12,16},{16,20},{20,24},{24,28},{1,5},{5,9},{9,... | collective-permute-start | bytes 1572872 | tf_op jit(solution)/shard_map/ppermute | solution.py:278
  120.0 10.8 %collective-permute-done.18.refs_1_ = f32[512,256]{1,0:T(8,128)S(1)} collective-permute-done((f32[512,256]{1,0:T(8,128)S(1)}, f32[512,256]{1,0:T(8,128)S(1)}, u32[]{:S(2)}, u32[]{:S(2)}) %collective-permute-start.18) | collective-permute-done | bytes 524320 | tf_op jit(solution)/shard_map/ppermute | solution.py:295
  131.0 1.1 maximum_add_fusion
  132.7 1.5 %join_parts.5 = f32[2048,256]{1,0:T(8,128)} custom-call(f32[512,256]{1,0:T(8,128)S(1)} %join_parts.4.refs_0_, f32[512,256]{1,0:T(8,128)S(1)} %collective-permute-done.18.refs_1_, f32[512,256]{1,0:T(8,128)S(1)} %collective-permute-done.19.refs_2_, f32[512,256]{1,0:T(8,128)S(1)} %collective-permute-done.20.refs_3_), custom_call_target="tpu_custom_call" | custom-call | tf_op jit(solution)/shard_map/join_parts/pallas_call | solution.py:333
  (43 shorter events, 2.3 us)
Async XLA Ops:
  0.6 20.8 %copy-start.7 = (s32[8,2]{0,1:T(2,128)S(1)}, s32[8,2]{0,1:T(2,128)}, u32[]{:S(2)}) copy-start(s32[8,2]{0,1:T(2,128)} %param.16) | copy-start | bytes 196
  1.9 17.6 %collective-permute-start.1 = (f32[2,256,256]{2,1,0:T(8,128)S(1)}, f32[2,256,256]{2,1,0:T(8,128)S(1)}, u32[]{:S(2)}, u32[]{:S(2)}) collective-permute-start(f32[2,256,256]{2,1,0:T(8,128)S(1)} %get-tuple-element.97), channel_id=1, source_target_pairs={{4,0},{8,4},{12,8},{16,12},{20,16},{24,20},{28,24},{5,1},{9,5},{13... | collective-permute-start | bytes 1572872 | tf_op jit(solution)/shard_map/ppermute | solution.py:278
  3.2 26.7 %collective-permute-start = (f32[2,256,256]{2,1,0:T(8,128)S(1)}, f32[2,256,256]{2,1,0:T(8,128)S(1)}, u32[]{:S(2)}, u32[]{:S(2)}) collective-permute-start(f32[2,256,256]{2,1,0:T(8,128)S(1)} %get-tuple-element.97), channel_id=1, source_target_pairs={{1,0},{2,1},{3,2},{5,4},{6,5},{7,6},{9,8},{10,9},{11,10},{13,12},{... | collective-permute-start | bytes 1572872 | tf_op jit(solution)/shard_map/ppermute | solution.py:278
  4.5 25.4 %collective-permute-start.2 = (f32[2,256,256]{2,1,0:T(8,128)S(1)}, f32[2,256,256]{2,1,0:T(8,128)S(1)}, u32[]{:S(2)}, u32[]{:S(2)}) collective-permute-start(f32[2,256,256]{2,1,0:T(8,128)S(1)} %get-tuple-element.96), channel_id=1, source_target_pairs={{4,0},{8,4},{12,8},{16,12},{20,16},{24,20},{28,24},{5,1},{9,5},{13... | collective-permute-start | bytes 1572872 | tf_op jit(solution)/shard_map/ppermute | solution.py:278
  19.5 10.4 %copy-start.3 = (f32[2,256,256]{2,1,0:T(8,128)}, f32[2,256,256]{2,1,0:T(8,128)S(1)}, u32[]{:S(2)}) copy-start(f32[2,256,256]{2,1,0:T(8,128)S(1)} %collective-permute-done.1.right) | copy-start | bytes 1572868
  19.5 10.4 %collective-permute-start.3 = (f32[2,256,256]{2,1,0:T(8,128)S(1)}, f32[2,256,256]{2,1,0:T(8,128)S(1)}, u32[]{:S(2)}, u32[]{:S(2)}) collective-permute-start(f32[2,256,256]{2,1,0:T(8,128)S(1)} %collective-permute-done.1.right), channel_id=1, source_target_pairs={{1,0},{2,1},{3,2},{5,4},{6,5},{7,6},{9,8},{10,9},{11,10},{13,12},{... | collective-permute-start | bytes 1572872 | tf_op jit(solution)/shard_map/ppermute | solution.py:278
  29.9 0.8 copy-start.5
  29.9 1.0 copy-start.4
  30.9 0.8 copy-start.6
  41.1 10.5 %collective-permute-start.4 = (f32[1024,256]{1,0:T(8,128)}, f32[1024,256]{1,0:T(8,128)S(1)}, u32[]{:S(2)}, u32[]{:S(2)}) collective-permute-start(f32[1024,256]{1,0:T(8,128)} %get-tuple-element.67), channel_id=1, source_target_pairs={{0,1},{1,0},{2,3},{3,2},{4,5},{5,4},{6,7},{7,6},{8,9},{9,8},{10,11... | collective-permute-start | bytes 3145736 | tf_op jit(solution)/shard_map/ppermute | solution.py:295
  47.2 22.8 %collective-permute-start.6 = (f32[2,256,256]{2,1,0:T(8,128)}, f32[2,256,256]{2,1,0:T(8,128)S(1)}, u32[]{:S(2)}, u32[]{:S(2)}) collective-permute-start(f32[2,256,256]{2,1,0:T(8,128)} %get-tuple-element.70), channel_id=1, source_target_pairs={{0,4},{4,8},{8,12},{12,16},{16,20},{20,24},{24,28},{1,5},{5,9},{9,... | collective-permute-start | bytes 1572872 | tf_op jit(solution)/shard_map/ppermute | solution.py:278
  51.6 1.2 copy-start
  52.8 38.6 %copy-start.9 = (f32[2,256,256]{2,1,0:T(8,128)S(1)}, f32[2,256,256]{2,1,0:T(8,128)}, u32[]{:S(2)}) copy-start(f32[2,256,256]{2,1,0:T(8,128)} %get-tuple-element.87) | copy-start | bytes 1572868
  52.8 40.0 %copy-start.8 = (f32[2,256,256]{2,1,0:T(8,128)S(1)}, f32[2,256,256]{2,1,0:T(8,128)}, u32[]{:S(2)}) copy-start(f32[2,256,256]{2,1,0:T(8,128)} %get-tuple-element.92) | copy-start | bytes 1572868
  52.8 59.2 %copy-start.2 = (f32[2,256,256]{2,1,0:T(8,128)S(1)}, f32[2,256,256]{2,1,0:T(8,128)}, u32[]{:S(2)}) copy-start(f32[2,256,256]{2,1,0:T(8,128)} %get-tuple-element.91) | copy-start | bytes 1572868
  52.9 29.3 %collective-permute-start.5 = (f32[512,256]{1,0:T(8,128)S(1)}, f32[512,256]{1,0:T(8,128)S(1)}, u32[]{:S(2)}, u32[]{:S(2)}) collective-permute-start(f32[512,256]{1,0:T(8,128)S(1)} %get-tuple-element.69), channel_id=1, source_target_pairs={{0,2},{1,3},{2,0},{3,1},{4,6},{5,7},{6,4},{7,5},{8,10},{9,11},{10,... | collective-permute-start | bytes 1572872 | tf_op jit(solution)/shard_map/ppermute | solution.py:295
  82.3 48.6 %copy-start.1 = (f32[2,512,256]{2,1,0:T(8,128)S(1)}, f32[2,512,256]{2,1,0:T(8,128)}, u32[]{:S(2)}) copy-start(f32[2,512,256]{2,1,0:T(8,128)} %get-tuple-element.65) | copy-start | bytes 3145732
  82.3 5.6 %collective-permute-start.7 = (f32[128,256]{1,0:T(8,128)S(1)}, f32[128,256]{1,0:T(8,128)S(1)}, u32[]{:S(2)}, u32[]{:S(2)}) collective-permute-start(f32[128,256]{1,0:T(8,128)S(1)} %get-tuple-element.79), channel_id=1, source_target_pairs={{0,4},{1,5},{2,6},{3,7},{4,0},{5,1},{6,2},{7,3},{8,12},{9,13},{10,... | collective-permute-start | bytes 393224 | tf_op jit(solution)/shard_map/ppermute | solution.py:295
  82.4 6.5 %collective-permute-start.8 = (f32[128,256]{1,0:T(8,128)S(1)}, f32[128,256]{1,0:T(8,128)S(1)}, u32[]{:S(2)}, u32[]{:S(2)}) collective-permute-start(f32[128,256]{1,0:T(8,128)S(1)} %get-tuple-element.80), channel_id=1, source_target_pairs={{0,8},{1,9},{2,10},{3,11},{4,12},{5,13},{6,14},{7,15},{8,0},{9,1},... | collective-permute-start | bytes 393224 | tf_op jit(solution)/shard_map/ppermute | solution.py:295
  82.5 8.9 %collective-permute-start.9 = (f32[128,256]{1,0:T(8,128)S(1)}, f32[128,256]{1,0:T(8,128)S(1)}, u32[]{:S(2)}, u32[]{:S(2)}) collective-permute-start(f32[128,256]{1,0:T(8,128)S(1)} %get-tuple-element.81), channel_id=1, source_target_pairs={{0,12},{1,13},{2,14},{3,15},{4,8},{5,9},{6,10},{7,11},{8,4},{9,5},... | collective-permute-start | bytes 393224 | tf_op jit(solution)/shard_map/ppermute | solution.py:295
  91.4 17.0 %collective-permute-start.12 = (f32[2,256,256]{2,1,0:T(8,128)S(1)}, f32[2,256,256]{2,1,0:T(8,128)S(1)}, u32[]{:S(2)}, u32[]{:S(2)}) collective-permute-start(f32[2,256,256]{2,1,0:T(8,128)S(1)} %copy-done.9), channel_id=1, source_target_pairs={{0,1},{1,2},{2,3},{4,5},{5,6},{6,7},{8,9},{9,10},{10,11},{12,13},{... | collective-permute-start | bytes 1572872 | tf_op jit(solution)/shard_map/ppermute | solution.py:278
  92.8 19.2 %collective-permute-start.16 = (f32[2,256,256]{2,1,0:T(8,128)S(1)}, f32[2,256,256]{2,1,0:T(8,128)S(1)}, u32[]{:S(2)}, u32[]{:S(2)}) collective-permute-start(f32[2,256,256]{2,1,0:T(8,128)S(1)} %copy-done.8), channel_id=1, source_target_pairs={{0,1},{1,2},{2,3},{4,5},{5,6},{6,7},{8,9},{9,10},{10,11},{12,13},{... | collective-permute-start | bytes 1572872 | tf_op jit(solution)/shard_map/ppermute | solution.py:278
  96.9 6.1 %collective-permute-start.10 = (f32[64,256]{1,0:T(8,128)S(1)}, f32[64,256]{1,0:T(8,128)S(1)}, u32[]{:S(2)}, u32[]{:S(2)}) collective-permute-start(f32[64,256]{1,0:T(8,128)S(1)} %get-tuple-element.86), channel_id=1, source_target_pairs={{0,16},{1,17},{2,18},{3,19},{4,20},{5,21},{6,22},{7,23},{8,24},{9,... | collective-permute-start | bytes 196616 | tf_op jit(solution)/shard_map/ppermute | solution.py:295
  102.9 5.5 %collective-permute-start.11 = (f32[64,256]{1,0:T(8,128)S(1)}, f32[64,256]{1,0:T(8,128)S(1)}, u32[]{:S(2)}, u32[]{:S(2)}) collective-permute-start(f32[64,256]{1,0:T(8,128)S(1)} %add_parts.7.refs_0_), channel_id=1, source_target_pairs={{0,16},{1,17},{2,18},{3,19},{4,20},{5,21},{6,22},{7,23},{8,24},{9,... | collective-permute-start | bytes 196616 | tf_op jit(solution)/shard_map/ppermute | solution.py:295
  108.5 7.4 %collective-permute-start.15 = (f32[128,256]{1,0:T(8,128)S(1)}, f32[128,256]{1,0:T(8,128)S(1)}, u32[]{:S(2)}, u32[]{:S(2)}) collective-permute-start(f32[128,256]{1,0:T(8,128)S(1)} %join_parts.3.refs_0_), channel_id=1, source_target_pairs={{0,12},{1,13},{2,14},{3,15},{4,8},{5,9},{6,10},{7,11},{8,4},{9,5},... | collective-permute-start | bytes 393224 | tf_op jit(solution)/shard_map/ppermute | solution.py:295
  108.5 7.7 %collective-permute-start.14 = (f32[128,256]{1,0:T(8,128)S(1)}, f32[128,256]{1,0:T(8,128)S(1)}, u32[]{:S(2)}, u32[]{:S(2)}) collective-permute-start(f32[128,256]{1,0:T(8,128)S(1)} %join_parts.3.refs_0_), channel_id=1, source_target_pairs={{0,8},{1,9},{2,10},{3,11},{4,12},{5,13},{6,14},{7,15},{8,0},{9,1},... | collective-permute-start | bytes 393224 | tf_op jit(solution)/shard_map/ppermute | solution.py:295
  110.5 6.8 %collective-permute-start.13 = (f32[128,256]{1,0:T(8,128)S(1)}, f32[128,256]{1,0:T(8,128)S(1)}, u32[]{:S(2)}, u32[]{:S(2)}) collective-permute-start(f32[128,256]{1,0:T(8,128)S(1)} %join_parts.3.refs_0_), channel_id=1, source_target_pairs={{0,4},{1,5},{2,6},{3,7},{4,0},{5,1},{6,2},{7,3},{8,12},{9,13},{10,... | collective-permute-start | bytes 393224 | tf_op jit(solution)/shard_map/ppermute | solution.py:295
  117.4 13.5 %collective-permute-start.18 = (f32[512,256]{1,0:T(8,128)S(1)}, f32[512,256]{1,0:T(8,128)S(1)}, u32[]{:S(2)}, u32[]{:S(2)}) collective-permute-start(f32[512,256]{1,0:T(8,128)S(1)} %join_parts.4.refs_0_), channel_id=1, source_target_pairs={{0,2},{1,3},{2,0},{3,1},{4,6},{5,7},{6,4},{7,5},{8,10},{9,11},{10,... | collective-permute-start | bytes 1572872 | tf_op jit(solution)/shard_map/ppermute | solution.py:295
  117.4 13.5 %collective-permute-start.17 = (f32[2,256,256]{2,1,0:T(8,128)S(1)}, f32[2,256,256]{2,1,0:T(8,128)S(1)}, u32[]{:S(2)}, u32[]{:S(2)}) collective-permute-start(f32[2,256,256]{2,1,0:T(8,128)S(1)} %add.20), channel_id=1, source_target_pairs={{0,4},{4,8},{8,12},{12,16},{16,20},{20,24},{24,28},{1,5},{5,9},{9,... | collective-permute-start | bytes 1572872 | tf_op jit(solution)/shard_map/ppermute | solution.py:278
  120.0 12.1 %collective-permute-start.19 = (f32[512,256]{1,0:T(8,128)S(1)}, f32[512,256]{1,0:T(8,128)S(1)}, u32[]{:S(2)}, u32[]{:S(2)}) collective-permute-start(f32[512,256]{1,0:T(8,128)S(1)} %join_parts.4.refs_0_), channel_id=1, source_target_pairs={{0,1},{1,0},{2,3},{3,2},{4,5},{5,4},{6,7},{7,6},{8,9},{9,8},{10,11... | collective-permute-start | bytes 1572872 | tf_op jit(solution)/shard_map/ppermute | solution.py:295
  130.8 1.9 %collective-permute-start.20 = (f32[512,256]{1,0:T(8,128)S(1)}, f32[512,256]{1,0:T(8,128)S(1)}, u32[]{:S(2)}, u32[]{:S(2)}) collective-permute-start(f32[512,256]{1,0:T(8,128)S(1)} %collective-permute-done.18.refs_1_), channel_id=1, source_target_pairs={{0,1},{1,0},{2,3},{3,2},{4,5},{5,4},{6,7},{7,6},{8,9},{9,8},{10,11... | collective-permute-start | bytes 1572872 | tf_op jit(solution)/shard_map/ppermute | solution.py:295

commit v2 on v1

--- a/solution.py
+++ b/solution.py
@@ -238,7 +238,8 @@
     order = jnp.asarray(parity_order(extent)).astype(BF16)
     smem = pl.BlockSpec(memory_space=pltpu.SMEM)
     vmem = pl.BlockSpec(memory_space=pltpu.VMEM)
-    hbm = pl.BlockSpec(memory_space=pl.ANY)
+    hbm = pl.BlockSpec(memory_space=pltpu.HBM)
+    anywhere = pl.BlockSpec(memory_space=pl.ANY)
     grad_shape = (2, tile_rows + extent, tile_cols + extent)
     sum_shape = (modes * 2 * extent, extent)
     half_sum = (sum_shape[0] // 2, extent)
@@ -247,8 +248,8 @@
     return pl.pallas_call(
         functools.partial(slots_kernel, tile_rows, tile_cols),
         out_shape=[jax.ShapeDtypeStruct(shape, F32) for shape in outs],
-        in_specs=[smem, smem] + [hbm] * 7 + [vmem, vmem],
-        out_specs=[hbm] * len(outs),
+        in_specs=[smem, smem, hbm] + [anywhere] * 4 + [hbm, hbm, vmem, vmem],
+        out_specs=[anywhere] * len(outs),
         scratch_shapes=[
             pltpu.VMEM(grad_shape, F32),
             pltpu.VMEM(grad_shape, F32),
@@ -267,7 +268,7 @@
             pltpu.SemaphoreType.DMA(()),
             pltpu.SemaphoreType.DMA((7,)),
         ],
-        compiler_params=pltpu.CompilerParams(vmem_limit_bytes=60 * 1024 * 1024),
+        compiler_params=pltpu.CompilerParams(vmem_limit_bytes=44 * 1024 * 1024),
         name="slots",
     )(offsets, live, own, below, right, right_low, corner, probe, amps, mats, order)
 

time: 133 us -> 128 us (0.962)
  the two profiles are of different devices: /device:TPU:0 before, /device:TPU:28 now
where the time goes in v2:
time: 128 us; the launch traced here: 129 us
  waiting for transfers between devices  64.8 us (51%)
  starting transfers between devices  46.9 us (37%)
  Pallas kernels  11.6 us (9%)
  local copies, waits for them, and re-layouts  2.49 us (2%)
  between operations  1.52 us (1%)
  other arithmetic  1.33 us (1%)
    ppermute x8, starting transfers between devices, shifted(): lax.ppermute(value, axis, [(source, source + steps) for source in range(f...  36.5 us
    ppermute x13, waiting for transfers between devices, swapped(): lax.ppermute(value, ('wide', 'narrow'), [(source, source ^ mask) for sour...  32.4 us
    ppermute x8, waiting for transfers between devices, shifted(): lax.ppermute(value, axis, [(source, source + steps) for source in range(f...  32.4 us
    ppermute x13, starting transfers between devices, swapped(): lax.ppermute(value, ('wide', 'narrow'), [(source, source ^ mask) for sour...  10.4 us
    pallas_call x1, Pallas kernels, run_slots(): pl.pallas_call(functools.partial(slots_kernel, tile_rows, tile_cols), out...  9.8 us
  transfers between devices with their start and end apart: 21, of which 14 were waited for; matrix products, arithmetic and copies ran while one was open for 1% of the time, Pallas kernels for 0%

profile of v2, /device:TPU:28, one launch (start us, length us, event | category | flops | bytes accessed | tf_op | source)
XLA Modules:
  0.0 128.6 jit_solution(12804315824939204420)
XLA Ops:
  0.7 2.4 %fusion = (f32[2,256,256]{2,1,0:T(8,128)}, f32[2,256,256]{2,1,0:T(8,128)}) fusion(f32[2,512,256]{2,1,0:T(8,128)} %own.1), kind=kLoop, calls=%fused_computation.2 | loop fusion | bytes 2097152 | tf_op jit(solution)/shard_map/slice | solution.py:384
  3.1 3.3 %collective-permute-start.1 = (f32[2,256,256]{2,1,0:T(8,128)}, f32[2,256,256]{2,1,0:T(8,128)S(1)}, u32[]{:S(2)}, u32[]{:S(2)}) collective-permute-start(f32[2,256,256]{2,1,0:T(8,128)} %get-tuple-element.97), channel_id=1, source_target_pairs={{4,0},{8,4},{12,8},{16,12},{20,16},{24,20},{28,24},{5,1},{9,5},{13... | collective-permute-start | bytes 1572872 | tf_op jit(solution)/shard_map/ppermute | solution.py:279
  6.3 1.9 %collective-permute-start = (f32[2,256,256]{2,1,0:T(8,128)}, f32[2,256,256]{2,1,0:T(8,128)S(1)}, u32[]{:S(2)}, u32[]{:S(2)}) collective-permute-start(f32[2,256,256]{2,1,0:T(8,128)} %get-tuple-element.97), channel_id=1, source_target_pairs={{1,0},{2,1},{3,2},{5,4},{6,5},{7,6},{9,8},{10,9},{11,10},{13,12},{... | collective-permute-start | bytes 1572872 | tf_op jit(solution)/shard_map/ppermute | solution.py:279
  8.3 2.4 %collective-permute-start.2 = (f32[2,256,256]{2,1,0:T(8,128)}, f32[2,256,256]{2,1,0:T(8,128)S(1)}, u32[]{:S(2)}, u32[]{:S(2)}) collective-permute-start(f32[2,256,256]{2,1,0:T(8,128)} %get-tuple-element.96), channel_id=1, source_target_pairs={{4,0},{8,4},{12,8},{16,12},{20,16},{24,20},{28,24},{5,1},{9,5},{13... | collective-permute-start | bytes 1572872 | tf_op jit(solution)/shard_map/ppermute | solution.py:279
  10.7 9.2 %collective-permute-done.1.right = f32[2,256,256]{2,1,0:T(8,128)S(1)} collective-permute-done((f32[2,256,256]{2,1,0:T(8,128)}, f32[2,256,256]{2,1,0:T(8,128)S(1)}, u32[]{:S(2)}, u32[]{:S(2)}) %collective-permute-start.1) | collective-permute-done | bytes 524320 | tf_op jit(solution)/shard_map/ppermute | solution.py:279
  20.0 1.9 %collective-permute-start.3 = (f32[2,256,256]{2,1,0:T(8,128)S(1)}, f32[2,256,256]{2,1,0:T(8,128)}, u32[]{:S(2)}, u32[]{:S(2)}) collective-permute-start(f32[2,256,256]{2,1,0:T(8,128)S(1)} %collective-permute-done.1.right), channel_id=1, source_target_pairs={{1,0},{2,1},{3,2},{5,4},{6,5},{7,6},{9,8},{10,9},{11,10},{13,12},{... | collective-permute-start | bytes 1572872 | tf_op jit(solution)/shard_map/ppermute | solution.py:279
  22.6 7.4 %collective-permute-done.2.right_low = f32[2,256,256]{2,1,0:T(8,128)S(1)} collective-permute-done((f32[2,256,256]{2,1,0:T(8,128)}, f32[2,256,256]{2,1,0:T(8,128)S(1)}, u32[]{:S(2)}, u32[]{:S(2)}) %collective-permute-start.2) | collective-permute-done | bytes 524320 | tf_op jit(solution)/shard_map/ppermute | solution.py:279
  30.1 9.8 %slots.1 = (f32[2,512,256]{2,1,0:T(8,128)S(1)}, f32[2,256,256]{2,1,0:T(8,128)S(1)}, f32[2,256,256]{2,1,0:T(8,128)S(1)}, f32[2,256,256]{2,1,0:T(8,128)S(1)}, f32[...) custom-call(s32[8,2]{1,0:T(8,128)S(1)} %copy.9.offsets, s32[1]{0:T(128)S(6)} %copy.11.live, ...), custom_call_target="tpu_custom_call" | custom-call | tf_op jit(solution)/shard_map/slots/pallas_call | solution.py:248
  40.0 20.4 %collective-permute-start.6 = (f32[2,256,256]{2,1,0:T(8,128)S(1)}, f32[2,256,256]{2,1,0:T(8,128)S(1)}, u32[]{:S(2)}, u32[]{:S(2)}) collective-permute-start(f32[2,256,256]{2,1,0:T(8,128)S(1)} %get-tuple-element.70), channel_id=1, source_target_pairs={{0,4},{4,8},{8,12},{12,16},{16,20},{20,24},{24,28},{1,5},{5,9},{9,... | collective-permute-start | bytes 1572872 | tf_op jit(solution)/shard_map/ppermute | solution.py:279
  60.4 0.1 add_parts.4
  60.6 11.6 %collective-permute-done.6 = f32[2,256,256]{2,1,0:T(8,128)S(1)} collective-permute-done((f32[2,256,256]{2,1,0:T(8,128)S(1)}, f32[2,256,256]{2,1,0:T(8,128)S(1)}, u32[]{:S(2)}, u32[]{:S(2)}) %collective-permute-start.6) | collective-permute-done | bytes 524320 | tf_op jit(solution)/shard_map/ppermute | solution.py:279
  72.2 2.4 %collective-permute-done.5.refs_1_ = f32[512,256]{1,0:T(8,128)S(1)} collective-permute-done((f32[512,256]{1,0:T(8,128)S(1)}, f32[512,256]{1,0:T(8,128)S(1)}, u32[]{:S(2)}, u32[]{:S(2)}) %collective-permute-start.5) | collective-permute-done | bytes 524320 | tf_op jit(solution)/shard_map/ppermute | solution.py:296
  74.7 0.7 collective-permute-start.7
  75.4 2.9 %collective-permute-start.9 = (f32[128,256]{1,0:T(8,128)S(1)}, f32[128,256]{1,0:T(8,128)S(1)}, u32[]{:S(2)}, u32[]{:S(2)}) collective-permute-start(f32[128,256]{1,0:T(8,128)S(1)} %get-tuple-element.81), channel_id=1, source_target_pairs={{0,12},{1,13},{2,14},{3,15},{4,8},{5,9},{6,10},{7,11},{8,4},{9,5},... | collective-permute-start | bytes 393224 | tf_op jit(solution)/shard_map/ppermute | solution.py:296
  78.3 2.4 %collective-permute-done.7.refs_1_ = f32[128,256]{1,0:T(8,128)S(1)} collective-permute-done((f32[128,256]{1,0:T(8,128)S(1)}, f32[128,256]{1,0:T(8,128)S(1)}, u32[]{:S(2)}, u32[]{:S(2)}) %collective-permute-start.7) | collective-permute-done | bytes 131104 | tf_op jit(solution)/shard_map/ppermute | solution.py:296
  80.7 0.6 collective-permute-done.8.refs_2_
  81.2 2.3 %collective-permute-done.9.refs_3_ = f32[128,256]{1,0:T(8,128)S(1)} collective-permute-done((f32[128,256]{1,0:T(8,128)S(1)}, f32[128,256]{1,0:T(8,128)S(1)}, u32[]{:S(2)}, u32[]{:S(2)}) %collective-permute-start.9) | collective-permute-done | bytes 131104 | tf_op jit(solution)/shard_map/ppermute | solution.py:296
  83.6 1.9 %collective-permute-start.12 = (f32[2,256,256]{2,1,0:T(8,128)S(1)}, f32[2,256,256]{2,1,0:T(8,128)S(1)}, u32[]{:S(2)}, u32[]{:S(2)}) collective-permute-start(f32[2,256,256]{2,1,0:T(8,128)S(1)} %get-tuple-element.87), channel_id=1, source_target_pairs={{0,1},{1,2},{2,3},{4,5},{5,6},{6,7},{8,9},{9,10},{10,11},{12,13},{... | collective-permute-start | bytes 1572872 | tf_op jit(solution)/shard_map/ppermute | solution.py:279
  85.5 1.9 %collective-permute-start.16 = (f32[2,256,256]{2,1,0:T(8,128)S(1)}, f32[2,256,256]{2,1,0:T(8,128)S(1)}, u32[]{:S(2)}, u32[]{:S(2)}) collective-permute-start(f32[2,256,256]{2,1,0:T(8,128)S(1)} %get-tuple-element.92), channel_id=1, source_target_pairs={{0,1},{1,2},{2,3},{4,5},{5,6},{6,7},{8,9},{9,10},{10,11},{12,13},{... | collective-permute-start | bytes 1572872 | tf_op jit(solution)/shard_map/ppermute | solution.py:279
  87.5 7.0 %collective-permute-done.10.refs_1_ = f32[64,256]{1,0:T(8,128)S(1)} collective-permute-done((f32[64,256]{1,0:T(8,128)S(1)}, f32[64,256]{1,0:T(8,128)S(1)}, u32[]{:S(2)}, u32[]{:S(2)}) %collective-permute-start.10) | collective-permute-done | bytes 65568 | tf_op jit(solution)/shard_map/ppermute | solution.py:296
  94.6 5.3 %collective-permute-done.11.refs_1_ = f32[64,256]{1,0:T(8,128)S(1)} collective-permute-done((f32[64,256]{1,0:T(8,128)S(1)}, f32[64,256]{1,0:T(8,128)S(1)}, u32[]{:S(2)}, u32[]{:S(2)}) %collective-permute-start.11) | collective-permute-done | bytes 65568 | tf_op jit(solution)/shard_map/ppermute | solution.py:296
  100.0 2.1 %collective-permute-start.14 = (f32[128,256]{1,0:T(8,128)S(1)}, f32[128,256]{1,0:T(8,128)S(1)}, u32[]{:S(2)}, u32[]{:S(2)}) collective-permute-start(f32[128,256]{1,0:T(8,128)S(1)} %join_parts.3.refs_0_), channel_id=1, source_target_pairs={{0,8},{1,9},{2,10},{3,11},{4,12},{5,13},{6,14},{7,15},{8,0},{9,1},... | collective-permute-start | bytes 393224 | tf_op jit(solution)/shard_map/ppermute | solution.py:296
  102.1 1.3 %collective-permute-start.13 = (f32[128,256]{1,0:T(8,128)S(1)}, f32[128,256]{1,0:T(8,128)S(1)}, u32[]{:S(2)}, u32[]{:S(2)}) collective-permute-start(f32[128,256]{1,0:T(8,128)S(1)} %join_parts.3.refs_0_), channel_id=1, source_target_pairs={{0,4},{1,5},{2,6},{3,7},{4,0},{5,1},{6,2},{7,3},{8,12},{9,13},{10,... | collective-permute-start | bytes 393224 | tf_op jit(solution)/shard_map/ppermute | solution.py:296
  103.5 2.3 %collective-permute-done.15.refs_3_ = f32[128,256]{1,0:T(8,128)S(1)} collective-permute-done((f32[128,256]{1,0:T(8,128)S(1)}, f32[128,256]{1,0:T(8,128)S(1)}, u32[]{:S(2)}, u32[]{:S(2)}) %collective-permute-start.15) | collective-permute-done | bytes 131104 | tf_op jit(solution)/shard_map/ppermute | solution.py:296
  105.8 0.6 collective-permute-done.14.refs_2_
  106.5 0.8 collective-permute-done.13.refs_1_
  107.3 2.9 %collective-permute-start.18 = (f32[512,256]{1,0:T(8,128)S(1)}, f32[512,256]{1,0:T(8,128)S(1)}, u32[]{:S(2)}, u32[]{:S(2)}) collective-permute-start(f32[512,256]{1,0:T(8,128)S(1)} %join_parts.4.refs_0_), channel_id=1, source_target_pairs={{0,2},{1,3},{2,0},{3,1},{4,6},{5,7},{6,4},{7,5},{8,10},{9,11},{10,... | collective-permute-start | bytes 1572872 | tf_op jit(solution)/shard_map/ppermute | solution.py:296
  110.2 2.7 %collective-permute-start.17 = (f32[2,256,256]{2,1,0:T(8,128)S(1)}, f32[2,256,256]{2,1,0:T(8,128)S(1)}, u32[]{:S(2)}, u32[]{:S(2)}) collective-permute-start(f32[2,256,256]{2,1,0:T(8,128)S(1)} %add.20), channel_id=1, source_target_pairs={{0,4},{4,8},{8,12},{12,16},{16,20},{20,24},{24,28},{1,5},{5,9},{9,... | collective-permute-start | bytes 1572872 | tf_op jit(solution)/shard_map/ppermute | solution.py:279
  113.0 8.8 %collective-permute-done.18.refs_1_ = f32[512,256]{1,0:T(8,128)S(1)} collective-permute-done((f32[512,256]{1,0:T(8,128)S(1)}, f32[512,256]{1,0:T(8,128)S(1)}, u32[]{:S(2)}, u32[]{:S(2)}) %collective-permute-start.18) | collective-permute-done | bytes 524320 | tf_op jit(solution)/shard_map/ppermute | solution.py:296
  121.9 4.1 %collective-permute-done.17 = f32[2,256,256]{2,1,0:T(8,128)S(1)} collective-permute-done((f32[2,256,256]{2,1,0:T(8,128)S(1)}, f32[2,256,256]{2,1,0:T(8,128)S(1)}, u32[]{:S(2)}, u32[]{:S(2)}) %collective-permute-start.17) | collective-permute-done | bytes 524320 | tf_op jit(solution)/shard_map/ppermute | solution.py:279
  126.0 1.1 maximum_add_fusion
  127.1 1.5 %join_parts.5 = f32[2048,256]{1,0:T(8,128)} custom-call(f32[512,256]{1,0:T(8,128)S(1)} %join_parts.4.refs_0_, f32[512,256]{1,0:T(8,128)S(1)} %collective-permute-done.18.refs_1_, f32[512,256]{1,0:T(8,128)S(1)} %collective-permute-done.19.refs_2_, f32[512,256]{1,0:T(8,128)S(1)} %collective-permute-done.20.refs_3_), custom_call_target="tpu_custom_call" | custom-call | tf_op jit(solution)/shard_map/join_parts/pallas_call | solution.py:334
  (31 shorter events, 0.9 us)
Async XLA Ops:
  0.6 29.4 %copy-start.2 = (bf16[256,256]{1,0:T(8,128)(2,1)S(1)}, bf16[256,256]{1,0:T(8,128)(2,1)}, u32[]{:S(2)}) copy-start(bf16[256,256]{1,0:T(8,128)(2,1)} %constant.71.order) | copy-start | bytes 393220
  0.6 29.4 %copy-start.1 = (bf16[2,2,256,256]{3,2,1,0:T(8,128)(2,1)S(1)}, bf16[2,2,256,256]{3,2,1,0:T(8,128)(2,1)}, u32[]{:S(2)}) copy-start(bf16[2,2,256,256]{3,2,1,0:T(8,128)(2,1)} %constant.66.clone.mats) | copy-start | bytes 1572868
  0.7 29.4 %copy-start = (f32[2,512,256]{2,1,0:T(8,128)S(1)}, f32[2,512,256]{2,1,0:T(8,128)}, u32[]{:S(2)}) copy-start(f32[2,512,256]{2,1,0:T(8,128)} %own.1) | copy-start | bytes 3145732
  0.7 21.9 %copy-start.3 = (s32[8,2]{0,1:T(2,128)S(1)}, s32[8,2]{0,1:T(2,128)}, u32[]{:S(2)}) copy-start(s32[8,2]{0,1:T(2,128)} %param.16) | copy-start | bytes 196
  3.1 16.9 %collective-permute-start.1 = (f32[2,256,256]{2,1,0:T(8,128)}, f32[2,256,256]{2,1,0:T(8,128)S(1)}, u32[]{:S(2)}, u32[]{:S(2)}) collective-permute-start(f32[2,256,256]{2,1,0:T(8,128)} %get-tuple-element.97), channel_id=1, source_target_pairs={{4,0},{8,4},{12,8},{16,12},{20,16},{24,20},{28,24},{5,1},{9,5},{13... | collective-permute-start | bytes 1572872 | tf_op jit(solution)/shard_map/ppermute | solution.py:279
  6.3 23.7 %collective-permute-start = (f32[2,256,256]{2,1,0:T(8,128)}, f32[2,256,256]{2,1,0:T(8,128)S(1)}, u32[]{:S(2)}, u32[]{:S(2)}) collective-permute-start(f32[2,256,256]{2,1,0:T(8,128)} %get-tuple-element.97), channel_id=1, source_target_pairs={{1,0},{2,1},{3,2},{5,4},{6,5},{7,6},{9,8},{10,9},{11,10},{13,12},{... | collective-permute-start | bytes 1572872 | tf_op jit(solution)/shard_map/ppermute | solution.py:279
  8.3 21.8 %collective-permute-start.2 = (f32[2,256,256]{2,1,0:T(8,128)}, f32[2,256,256]{2,1,0:T(8,128)S(1)}, u32[]{:S(2)}, u32[]{:S(2)}) collective-permute-start(f32[2,256,256]{2,1,0:T(8,128)} %get-tuple-element.96), channel_id=1, source_target_pairs={{4,0},{8,4},{12,8},{16,12},{20,16},{24,20},{28,24},{5,1},{9,5},{13... | collective-permute-start | bytes 1572872 | tf_op jit(solution)/shard_map/ppermute | solution.py:279
  20.0 10.1 %collective-permute-start.3 = (f32[2,256,256]{2,1,0:T(8,128)S(1)}, f32[2,256,256]{2,1,0:T(8,128)}, u32[]{:S(2)}, u32[]{:S(2)}) collective-permute-start(f32[2,256,256]{2,1,0:T(8,128)S(1)} %collective-permute-done.1.right), channel_id=1, source_target_pairs={{1,0},{2,1},{3,2},{5,4},{6,5},{7,6},{9,8},{10,9},{11,10},{13,12},{... | collective-permute-start | bytes 1572872 | tf_op jit(solution)/shard_map/ppermute | solution.py:279
  39.9 20.5 %collective-permute-start.4 = (f32[1024,256]{1,0:T(8,128)S(1)}, f32[1024,256]{1,0:T(8,128)S(1)}, u32[]{:S(2)}, u32[]{:S(2)}) collective-permute-start(f32[1024,256]{1,0:T(8,128)S(1)} %get-tuple-element.67), channel_id=1, source_target_pairs={{0,1},{1,0},{2,3},{3,2},{4,5},{5,4},{6,7},{7,6},{8,9},{9,8},{10,11... | collective-permute-start | bytes 3145736 | tf_op jit(solution)/shard_map/ppermute | solution.py:296
  40.0 32.3 %collective-permute-start.6 = (f32[2,256,256]{2,1,0:T(8,128)S(1)}, f32[2,256,256]{2,1,0:T(8,128)S(1)}, u32[]{:S(2)}, u32[]{:S(2)}) collective-permute-start(f32[2,256,256]{2,1,0:T(8,128)S(1)} %get-tuple-element.70), channel_id=1, source_target_pairs={{0,4},{4,8},{8,12},{12,16},{16,20},{20,24},{24,28},{1,5},{5,9},{9,... | collective-permute-start | bytes 1572872 | tf_op jit(solution)/shard_map/ppermute | solution.py:279
  60.6 14.1 %collective-permute-start.5 = (f32[512,256]{1,0:T(8,128)S(1)}, f32[512,256]{1,0:T(8,128)S(1)}, u32[]{:S(2)}, u32[]{:S(2)}) collective-permute-start(f32[512,256]{1,0:T(8,128)S(1)} %get-tuple-element.69), channel_id=1, source_target_pairs={{0,2},{1,3},{2,0},{3,1},{4,6},{5,7},{6,4},{7,5},{8,10},{9,11},{10,... | collective-permute-start | bytes 1572872 | tf_op jit(solution)/shard_map/ppermute | solution.py:296
  74.7 6.0 %collective-permute-start.7 = (f32[128,256]{1,0:T(8,128)S(1)}, f32[128,256]{1,0:T(8,128)S(1)}, u32[]{:S(2)}, u32[]{:S(2)}) collective-permute-start(f32[128,256]{1,0:T(8,128)S(1)} %get-tuple-element.79), channel_id=1, source_target_pairs={{0,4},{1,5},{2,6},{3,7},{4,0},{5,1},{6,2},{7,3},{8,12},{9,13},{10,... | collective-permute-start | bytes 393224 | tf_op jit(solution)/shard_map/ppermute | solution.py:296
  75.4 5.8 %collective-permute-start.8 = (f32[128,256]{1,0:T(8,128)S(1)}, f32[128,256]{1,0:T(8,128)S(1)}, u32[]{:S(2)}, u32[]{:S(2)}) collective-permute-start(f32[128,256]{1,0:T(8,128)S(1)} %get-tuple-element.80), channel_id=1, source_target_pairs={{0,8},{1,9},{2,10},{3,11},{4,12},{5,13},{6,14},{7,15},{8,0},{9,1},... | collective-permute-start | bytes 393224 | tf_op jit(solution)/shard_map/ppermute | solution.py:296
  75.4 8.1 %collective-permute-start.9 = (f32[128,256]{1,0:T(8,128)S(1)}, f32[128,256]{1,0:T(8,128)S(1)}, u32[]{:S(2)}, u32[]{:S(2)}) collective-permute-start(f32[128,256]{1,0:T(8,128)S(1)} %get-tuple-element.81), channel_id=1, source_target_pairs={{0,12},{1,13},{2,14},{3,15},{4,8},{5,9},{6,10},{7,11},{8,4},{9,5},... | collective-permute-start | bytes 393224 | tf_op jit(solution)/shard_map/ppermute | solution.py:296
  83.6 16.3 %collective-permute-start.12 = (f32[2,256,256]{2,1,0:T(8,128)S(1)}, f32[2,256,256]{2,1,0:T(8,128)S(1)}, u32[]{:S(2)}, u32[]{:S(2)}) collective-permute-start(f32[2,256,256]{2,1,0:T(8,128)S(1)} %get-tuple-element.87), channel_id=1, source_target_pairs={{0,1},{1,2},{2,3},{4,5},{5,6},{6,7},{8,9},{9,10},{10,11},{12,13},{... | collective-permute-start | bytes 1572872 | tf_op jit(solution)/shard_map/ppermute | solution.py:279
  85.5 17.9 %collective-permute-start.16 = (f32[2,256,256]{2,1,0:T(8,128)S(1)}, f32[2,256,256]{2,1,0:T(8,128)S(1)}, u32[]{:S(2)}, u32[]{:S(2)}) collective-permute-start(f32[2,256,256]{2,1,0:T(8,128)S(1)} %get-tuple-element.92), channel_id=1, source_target_pairs={{0,1},{1,2},{2,3},{4,5},{5,6},{6,7},{8,9},{9,10},{10,11},{12,13},{... | collective-permute-start | bytes 1572872 | tf_op jit(solution)/shard_map/ppermute | solution.py:279
  87.4 7.1 %collective-permute-start.10 = (f32[64,256]{1,0:T(8,128)S(1)}, f32[64,256]{1,0:T(8,128)S(1)}, u32[]{:S(2)}, u32[]{:S(2)}) collective-permute-start(f32[64,256]{1,0:T(8,128)S(1)} %get-tuple-element.86), channel_id=1, source_target_pairs={{0,16},{1,17},{2,18},{3,19},{4,20},{5,21},{6,22},{7,23},{8,24},{9,... | collective-permute-start | bytes 196616 | tf_op jit(solution)/shard_map/ppermute | solution.py:296
  94.5 5.3 %collective-permute-start.11 = (f32[64,256]{1,0:T(8,128)S(1)}, f32[64,256]{1,0:T(8,128)S(1)}, u32[]{:S(2)}, u32[]{:S(2)}) collective-permute-start(f32[64,256]{1,0:T(8,128)S(1)} %add_parts.7.refs_0_), channel_id=1, source_target_pairs={{0,16},{1,17},{2,18},{3,19},{4,20},{5,21},{6,22},{7,23},{8,24},{9,... | collective-permute-start | bytes 196616 | tf_op jit(solution)/shard_map/ppermute | solution.py:296
  99.9 5.9 %collective-permute-start.15 = (f32[128,256]{1,0:T(8,128)S(1)}, f32[128,256]{1,0:T(8,128)S(1)}, u32[]{:S(2)}, u32[]{:S(2)}) collective-permute-start(f32[128,256]{1,0:T(8,128)S(1)} %join_parts.3.refs_0_), channel_id=1, source_target_pairs={{0,12},{1,13},{2,14},{3,15},{4,8},{5,9},{6,10},{7,11},{8,4},{9,5},... | collective-permute-start | bytes 393224 | tf_op jit(solution)/shard_map/ppermute | solution.py:296
  100.0 6.5 %collective-permute-start.14 = (f32[128,256]{1,0:T(8,128)S(1)}, f32[128,256]{1,0:T(8,128)S(1)}, u32[]{:S(2)}, u32[]{:S(2)}) collective-permute-start(f32[128,256]{1,0:T(8,128)S(1)} %join_parts.3.refs_0_), channel_id=1, source_target_pairs={{0,8},{1,9},{2,10},{3,11},{4,12},{5,13},{6,14},{7,15},{8,0},{9,1},... | collective-permute-start | bytes 393224 | tf_op jit(solution)/shard_map/ppermute | solution.py:296
  102.1 5.1 %collective-permute-start.13 = (f32[128,256]{1,0:T(8,128)S(1)}, f32[128,256]{1,0:T(8,128)S(1)}, u32[]{:S(2)}, u32[]{:S(2)}) collective-permute-start(f32[128,256]{1,0:T(8,128)S(1)} %join_parts.3.refs_0_), channel_id=1, source_target_pairs={{0,4},{1,5},{2,6},{3,7},{4,0},{5,1},{6,2},{7,3},{8,12},{9,13},{10,... | collective-permute-start | bytes 393224 | tf_op jit(solution)/shard_map/ppermute | solution.py:296
  107.3 14.5 %collective-permute-start.18 = (f32[512,256]{1,0:T(8,128)S(1)}, f32[512,256]{1,0:T(8,128)S(1)}, u32[]{:S(2)}, u32[]{:S(2)}) collective-permute-start(f32[512,256]{1,0:T(8,128)S(1)} %join_parts.4.refs_0_), channel_id=1, source_target_pairs={{0,2},{1,3},{2,0},{3,1},{4,6},{5,7},{6,4},{7,5},{8,10},{9,11},{10,... | collective-permute-start | bytes 1572872 | tf_op jit(solution)/shard_map/ppermute | solution.py:296
  110.2 15.8 %collective-permute-start.17 = (f32[2,256,256]{2,1,0:T(8,128)S(1)}, f32[2,256,256]{2,1,0:T(8,128)S(1)}, u32[]{:S(2)}, u32[]{:S(2)}) collective-permute-start(f32[2,256,256]{2,1,0:T(8,128)S(1)} %add.20), channel_id=1, source_target_pairs={{0,4},{4,8},{8,12},{12,16},{16,20},{20,24},{24,28},{1,5},{5,9},{9,... | collective-permute-start | bytes 1572872 | tf_op jit(solution)/shard_map/ppermute | solution.py:279
  112.9 14.2 %collective-permute-start.19 = (f32[512,256]{1,0:T(8,128)S(1)}, f32[512,256]{1,0:T(8,128)S(1)}, u32[]{:S(2)}, u32[]{:S(2)}) collective-permute-start(f32[512,256]{1,0:T(8,128)S(1)} %join_parts.4.refs_0_), channel_id=1, source_target_pairs={{0,1},{1,0},{2,3},{3,2},{4,5},{5,4},{6,7},{7,6},{8,9},{9,8},{10,11... | collective-permute-start | bytes 1572872 | tf_op jit(solution)/shard_map/ppermute | solution.py:296
  121.8 5.4 %collective-permute-start.20 = (f32[512,256]{1,0:T(8,128)S(1)}, f32[512,256]{1,0:T(8,128)S(1)}, u32[]{:S(2)}, u32[]{:S(2)}) collective-permute-start(f32[512,256]{1,0:T(8,128)S(1)} %collective-permute-done.18.refs_1_), channel_id=1, source_target_pairs={{0,1},{1,0},{2,3},{3,2},{4,5},{5,4},{6,7},{7,6},{8,9},{9,8},{10,11... | collective-permute-start | bytes 1572872 | tf_op jit(solution)/shard_map/ppermute | solution.py:296

commit v3 on v2

--- a/solution.py
+++ b/solution.py
@@ -345,35 +345,25 @@
     return lax.optimization_barrier(values)
 
 
-def sum_and_shift(keep, send, scale, grad_below, grad_right, grad_right_low, grad_corner):
+def sum_everywhere(keep, send, scale, first, second):
     narrow, wide = lax.axis_size("narrow"), lax.axis_size("wide")
     bits = [1 << n for n in range((narrow * wide).bit_length() - 1)]
     groups = [(bits[1],)] + [tuple(bits[n : n + 2]) for n in range(2, len(bits), 2)]
     parts = [keep, swapped(send, bits[0])]
-    came_right_low = shifted(grad_right_low, "wide", 1)
     for n, group in enumerate(groups):
         pieces = add_parts(parts, group)
-        if n == 1:
-            pieces, grad_corner = together(pieces, grad_corner)
-            came_corner = shifted(grad_corner, "narrow", 1)
-        if n == 2:
-            pieces, grad_below = together(pieces, grad_below)
-            came_below = shifted(grad_below, "narrow", 1)
         parts = [pieces[0]] + [swapped(piece, mask) for piece, mask in zip(pieces[1:], partners(group)[1:])]
         if n == 0:
-            parts, came_right_low = together(parts, came_right_low)
+            parts, first = together(parts, first)
     value = add_parts(parts, ())[0]
     for group in reversed(groups):
         if group == groups[0]:
-            value, grad_right = together(value, grad_right + came_corner)
-            came_right = shifted(grad_right, "wide", 1)
+            value, second = together(value, second)
         parts = [value] + [swapped(value, mask) for mask in partners(group)[1:]]
-        if group == groups[-1]:
-            parts, came_below = together(parts, came_below)
         if group != groups[0]:
             value = join_parts(parts, group)
     parts = parts + [swapped(part, bits[0]) for part in parts]
-    return join_parts(parts, groups[0] + (bits[0],), scale), came_below, came_right, came_right_low
+    return join_parts(parts, groups[0] + (bits[0],), scale), first, second
 
 
 def on_device(object_field, probe, amplitudes, offsets, live):
@@ -386,9 +376,13 @@
     grad_own, grad_below, grad_right, grad_right_low, grad_corner, keep, send = run_slots(
         offsets, live, object_field, below, right, right_low, corner, probe, amplitudes
     )
+    came_right_low = shifted(grad_right_low, "wide", 1)
+    grad_right, send = together(grad_right + shifted(grad_corner, "narrow", 1), send)
+    came_below = shifted(grad_below, "narrow", 1)
+    came_right = shifted(grad_right, "wide", 1)
     total_slots = lax.axis_size("wide") * lax.axis_size("narrow") * offsets.shape[0]
-    probe_grad, came_below, came_right, came_right_low = sum_and_shift(
-        keep, send, 1.0 / math.sqrt(total_slots), grad_below, grad_right, grad_right_low, grad_corner
+    probe_grad, came_right_low, (came_right, came_below) = sum_everywhere(
+        keep, send, 1.0 / math.sqrt(total_slots), came_right_low, (came_right, came_below)
     )
     rims = jnp.concatenate([came_right, came_right_low], 1)
     object_grad = grad_own.at[:, :extent, :].add(came_below).at[:, :, :extent].add(rims)

time: 128 us -> 138 us (1.078)
  the two profiles are of different devices: /device:TPU:28 before, /device:TPU:0 now
where the time goes in v3:
time: 138 us; the launch traced here: 137 us
  starting transfers between devices  65.8 us (48%)
  waiting for transfers between devices  54 us (39%)
  Pallas kernels  11.6 us (8%)
  local copies, waits for them, and re-layouts  2.49 us (2%)
  between operations  1.52 us (1%)
    ppermute x13, starting transfers between devices, swapped(): lax.ppermute(value, ('wide', 'narrow'), [(source, source ^ mask) for sour...  33.5 us
    ppermute x8, starting transfers between devices, shifted(): lax.ppermute(value, axis, [(source, source + steps) for source in range(f...  32.3 us
    ppermute x13, waiting for transfers between devices, swapped(): lax.ppermute(value, ('wide', 'narrow'), [(source, source ^ mask) for sour...  30.2 us
    ppermute x8, waiting for transfers between devices, shifted(): lax.ppermute(value, axis, [(source, source + steps) for source in range(f...  23.8 us
    pallas_call x1, Pallas kernels, run_slots(): pl.pallas_call(functools.partial(slots_kernel, tile_rows, tile_cols), out...  9.8 us
  transfers between devices with their start and end apart: 21, of which 11 were waited for; matrix products, arithmetic and copies ran while one was open for 1% of the time, Pallas kernels for 0%

profile of v3, /device:TPU:0, one launch (start us, length us, event | category | flops | bytes accessed | tf_op | source)
XLA Modules:
  0.0 136.7 jit_solution(144757789315179240)
XLA Ops:
  0.7 2.4 %fusion = (f32[2,256,256]{2,1,0:T(8,128)}, f32[2,256,256]{2,1,0:T(8,128)}) fusion(f32[2,512,256]{2,1,0:T(8,128)} %own.1), kind=kLoop, calls=%fused_computation.2 | loop fusion | bytes 2097152 | tf_op jit(solution)/shard_map/slice | solution.py:374
  3.1 1.3 collective-permute-start.1
  4.3 1.3 collective-permute-start
  5.6 1.3 collective-permute-start.2
  6.9 13.9 %collective-permute-done.1.right = f32[2,256,256]{2,1,0:T(8,128)S(1)} collective-permute-done((f32[2,256,256]{2,1,0:T(8,128)}, f32[2,256,256]{2,1,0:T(8,128)S(1)}, u32[]{:S(2)}, u32[]{:S(2)}) %collective-permute-start.1) | collective-permute-done | bytes 524320 | tf_op jit(solution)/shard_map/ppermute | solution.py:279
  20.8 1.3 collective-permute-start.3
  22.9 8.4 %collective-permute-done.2.right_low = f32[2,256,256]{2,1,0:T(8,128)S(1)} collective-permute-done((f32[2,256,256]{2,1,0:T(8,128)}, f32[2,256,256]{2,1,0:T(8,128)S(1)}, u32[]{:S(2)}, u32[]{:S(2)}) %collective-permute-start.2) | collective-permute-done | bytes 524320 | tf_op jit(solution)/shard_map/ppermute | solution.py:279
  31.3 9.8 %slots.1 = (f32[2,512,256]{2,1,0:T(8,128)S(1)}, f32[2,256,256]{2,1,0:T(8,128)S(1)}, f32[2,256,256]{2,1,0:T(8,128)S(1)}, f32[2,256,256]{2,1,0:T(8,128)S(1)}, f32[...) custom-call(s32[8,2]{1,0:T(8,128)S(1)} %copy.9.offsets, s32[1]{0:T(128)S(6)} %copy.11.live, ...), custom_call_target="tpu_custom_call" | custom-call | tf_op jit(solution)/shard_map/slots/pallas_call | solution.py:248
  41.1 2.5 %collective-permute-start.4 = (f32[2,256,256]{2,1,0:T(8,128)S(1)}, f32[2,256,256]{2,1,0:T(8,128)S(1)}, u32[]{:S(2)}, u32[]{:S(2)}) collective-permute-start(f32[2,256,256]{2,1,0:T(8,128)S(1)} %get-tuple-element.60), channel_id=1, source_target_pairs={{0,1},{1,2},{2,3},{4,5},{5,6},{6,7},{8,9},{9,10},{10,11},{12,13},{... | collective-permute-start | bytes 1572872 | tf_op jit(solution)/shard_map/ppermute | solution.py:279
  43.6 1.5 %collective-permute-done.4 = f32[2,256,256]{2,1,0:T(8,128)S(1)} collective-permute-done((f32[2,256,256]{2,1,0:T(8,128)S(1)}, f32[2,256,256]{2,1,0:T(8,128)S(1)}, u32[]{:S(2)}, u32[]{:S(2)}) %collective-permute-start.4) | collective-permute-done | bytes 524320 | tf_op jit(solution)/shard_map/ppermute | solution.py:279
  45.2 9.1 %collective-permute-start.5 = (f32[1024,256]{1,0:T(8,128)S(1)}, f32[1024,256]{1,0:T(8,128)S(1)}, u32[]{:S(2)}, u32[]{:S(2)}) collective-permute-start(f32[1024,256]{1,0:T(8,128)S(1)} %get-tuple-element.62), channel_id=1, source_target_pairs={{0,1},{1,0},{2,3},{3,2},{4,5},{5,4},{6,7},{7,6},{8,9},{9,8},{10,11... | collective-permute-start | bytes 3145736 | tf_op jit(solution)/shard_map/ppermute | solution.py:296
  54.3 3.1 %collective-permute-start.7 = (f32[2,256,256]{2,1,0:T(8,128)S(1)}, f32[2,256,256]{2,1,0:T(8,128)S(1)}, u32[]{:S(2)}, u32[]{:S(2)}) collective-permute-start(f32[2,256,256]{2,1,0:T(8,128)S(1)} %get-tuple-element.65), channel_id=1, source_target_pairs={{0,4},{4,8},{8,12},{12,16},{16,20},{20,24},{24,28},{1,5},{5,9},{9,... | collective-permute-start | bytes 1572872 | tf_op jit(solution)/shard_map/ppermute | solution.py:279
  57.4 0.1 add_parts.4
  57.6 2.5 %collective-permute-start.6 = (f32[512,256]{1,0:T(8,128)S(1)}, f32[512,256]{1,0:T(8,128)S(1)}, u32[]{:S(2)}, u32[]{:S(2)}) collective-permute-start(f32[512,256]{1,0:T(8,128)S(1)} %get-tuple-element.64), channel_id=1, source_target_pairs={{0,2},{1,3},{2,0},{3,1},{4,6},{5,7},{6,4},{7,5},{8,10},{9,11},{10,... | collective-permute-start | bytes 1572872 | tf_op jit(solution)/shard_map/ppermute | solution.py:296
  60.0 1.8 %collective-permute-start.17 = (f32[2,256,256]{2,1,0:T(8,128)S(1)}, f32[2,256,256]{2,1,0:T(8,128)S(1)}, u32[]{:S(2)}, u32[]{:S(2)}) collective-permute-start(f32[2,256,256]{2,1,0:T(8,128)S(1)} %get-tuple-element.75), channel_id=1, source_target_pairs={{0,1},{1,2},{2,3},{4,5},{5,6},{6,7},{8,9},{9,10},{10,11},{12,13},{... | collective-permute-start | bytes 1572872 | tf_op jit(solution)/shard_map/ppermute | solution.py:279
  61.9 19.6 %collective-permute-start.16 = (f32[2,256,256]{2,1,0:T(8,128)S(1)}, f32[2,256,256]{2,1,0:T(8,128)S(1)}, u32[]{:S(2)}, u32[]{:S(2)}) collective-permute-start(f32[2,256,256]{2,1,0:T(8,128)S(1)} %add.19), channel_id=1, source_target_pairs={{0,4},{4,8},{8,12},{12,16},{16,20},{20,24},{24,28},{1,5},{5,9},{9,... | collective-permute-start | bytes 1572872 | tf_op jit(solution)/shard_map/ppermute | solution.py:279
  81.6 8.5 %collective-permute-start.8 = (f32[128,256]{1,0:T(8,128)S(1)}, f32[128,256]{1,0:T(8,128)S(1)}, u32[]{:S(2)}, u32[]{:S(2)}) collective-permute-start(f32[128,256]{1,0:T(8,128)S(1)} %get-tuple-element.69), channel_id=1, source_target_pairs={{0,4},{1,5},{2,6},{3,7},{4,0},{5,1},{6,2},{7,3},{8,12},{9,13},{10,... | collective-permute-start | bytes 393224 | tf_op jit(solution)/shard_map/ppermute | solution.py:296
  90.1 1.5 %collective-permute-start.10 = (f32[128,256]{1,0:T(8,128)S(1)}, f32[128,256]{1,0:T(8,128)S(1)}, u32[]{:S(2)}, u32[]{:S(2)}) collective-permute-start(f32[128,256]{1,0:T(8,128)S(1)} %get-tuple-element.71), channel_id=1, source_target_pairs={{0,12},{1,13},{2,14},{3,15},{4,8},{5,9},{6,10},{7,11},{8,4},{9,5},... | collective-permute-start | bytes 393224 | tf_op jit(solution)/shard_map/ppermute | solution.py:296
  91.6 6.9 %collective-permute-done.8.refs_1_ = f32[128,256]{1,0:T(8,128)S(1)} collective-permute-done((f32[128,256]{1,0:T(8,128)S(1)}, f32[128,256]{1,0:T(8,128)S(1)}, u32[]{:S(2)}, u32[]{:S(2)}) %collective-permute-start.8) | collective-permute-done | bytes 131104 | tf_op jit(solution)/shard_map/ppermute | solution.py:296
  98.7 5.2 %collective-permute-done.11.refs_1_ = f32[64,256]{1,0:T(8,128)S(1)} collective-permute-done((f32[64,256]{1,0:T(8,128)S(1)}, f32[64,256]{1,0:T(8,128)S(1)}, u32[]{:S(2)}, u32[]{:S(2)}) %collective-permute-start.11) | collective-permute-done | bytes 65568 | tf_op jit(solution)/shard_map/ppermute | solution.py:296
  103.9 5.2 %collective-permute-done.12.refs_1_ = f32[64,256]{1,0:T(8,128)S(1)} collective-permute-done((f32[64,256]{1,0:T(8,128)S(1)}, f32[64,256]{1,0:T(8,128)S(1)}, u32[]{:S(2)}, u32[]{:S(2)}) %collective-permute-start.12) | collective-permute-done | bytes 65568 | tf_op jit(solution)/shard_map/ppermute | solution.py:296
  109.1 6.2 %collective-permute-start.15 = (f32[128,256]{1,0:T(8,128)S(1)}, f32[128,256]{1,0:T(8,128)S(1)}, u32[]{:S(2)}, u32[]{:S(2)}) collective-permute-start(f32[128,256]{1,0:T(8,128)S(1)} %join_parts.3.refs_0_), channel_id=1, source_target_pairs={{0,12},{1,13},{2,14},{3,15},{4,8},{5,9},{6,10},{7,11},{8,4},{9,5},... | collective-permute-start | bytes 393224 | tf_op jit(solution)/shard_map/ppermute | solution.py:296
  115.3 1.6 %collective-permute-start.14 = (f32[128,256]{1,0:T(8,128)S(1)}, f32[128,256]{1,0:T(8,128)S(1)}, u32[]{:S(2)}, u32[]{:S(2)}) collective-permute-start(f32[128,256]{1,0:T(8,128)S(1)} %join_parts.3.refs_0_), channel_id=1, source_target_pairs={{0,8},{1,9},{2,10},{3,11},{4,12},{5,13},{6,14},{7,15},{8,0},{9,1},... | collective-permute-start | bytes 393224 | tf_op jit(solution)/shard_map/ppermute | solution.py:296
  116.9 1.1 collective-permute-start.13
  118.0 0.7 collective-permute-done.15.refs_3_
  118.7 2.5 %collective-permute-done.14.refs_2_ = f32[128,256]{1,0:T(8,128)S(1)} collective-permute-done((f32[128,256]{1,0:T(8,128)S(1)}, f32[128,256]{1,0:T(8,128)S(1)}, u32[]{:S(2)}, u32[]{:S(2)}) %collective-permute-start.14) | collective-permute-done | bytes 131104 | tf_op jit(solution)/shard_map/ppermute | solution.py:296
  121.2 0.6 collective-permute-done.13.refs_1_
  121.9 2.9 %collective-permute-start.18 = (f32[512,256]{1,0:T(8,128)S(1)}, f32[512,256]{1,0:T(8,128)S(1)}, u32[]{:S(2)}, u32[]{:S(2)}) collective-permute-start(f32[512,256]{1,0:T(8,128)S(1)} %join_parts.4.refs_0_), channel_id=1, source_target_pairs={{0,2},{1,3},{2,0},{3,1},{4,6},{5,7},{6,4},{7,5},{8,10},{9,11},{10,... | collective-permute-start | bytes 1572872 | tf_op jit(solution)/shard_map/ppermute | solution.py:296
  124.8 8.4 %collective-permute-done.18.refs_1_ = f32[512,256]{1,0:T(8,128)S(1)} collective-permute-done((f32[512,256]{1,0:T(8,128)S(1)}, f32[512,256]{1,0:T(8,128)S(1)}, u32[]{:S(2)}, u32[]{:S(2)}) %collective-permute-start.18) | collective-permute-done | bytes 524320 | tf_op jit(solution)/shard_map/ppermute | solution.py:296
  133.4 1.1 maximum_add_fusion
  134.5 0.7 collective-permute-done.20.refs_3_
  135.2 1.5 %join_parts.5 = f32[2048,256]{1,0:T(8,128)} custom-call(f32[512,256]{1,0:T(8,128)S(1)} %join_parts.4.refs_0_, f32[512,256]{1,0:T(8,128)S(1)} %collective-permute-done.18.refs_1_, f32[512,256]{1,0:T(8,128)S(1)} %collective-permute-done.19.refs_2_, f32[512,256]{1,0:T(8,128)S(1)} %collective-permute-done.20.refs_3_), custom_call_target="tpu_custom_call" | custom-call | tf_op jit(solution)/shard_map/join_parts/pallas_call | solution.py:334
  (31 shorter events, 0.7 us)
Async XLA Ops:
  0.6 30.6 %copy-start.2 = (bf16[256,256]{1,0:T(8,128)(2,1)S(1)}, bf16[256,256]{1,0:T(8,128)(2,1)}, u32[]{:S(2)}) copy-start(bf16[256,256]{1,0:T(8,128)(2,1)} %constant.71.order) | copy-start | bytes 393220
  0.6 30.6 %copy-start.1 = (bf16[2,2,256,256]{3,2,1,0:T(8,128)(2,1)S(1)}, bf16[2,2,256,256]{3,2,1,0:T(8,128)(2,1)}, u32[]{:S(2)}) copy-start(bf16[2,2,256,256]{3,2,1,0:T(8,128)(2,1)} %constant.66.clone.mats) | copy-start | bytes 1572868
  0.7 30.6 %copy-start = (f32[2,512,256]{2,1,0:T(8,128)S(1)}, f32[2,512,256]{2,1,0:T(8,128)}, u32[]{:S(2)}) copy-start(f32[2,512,256]{2,1,0:T(8,128)} %own.1) | copy-start | bytes 3145732
  0.7 22.1 %copy-start.3 = (s32[8,2]{0,1:T(2,128)S(1)}, s32[8,2]{0,1:T(2,128)}, u32[]{:S(2)}) copy-start(s32[8,2]{0,1:T(2,128)} %param.16) | copy-start | bytes 196
  3.1 17.8 %collective-permute-start.1 = (f32[2,256,256]{2,1,0:T(8,128)}, f32[2,256,256]{2,1,0:T(8,128)S(1)}, u32[]{:S(2)}, u32[]{:S(2)}) collective-permute-start(f32[2,256,256]{2,1,0:T(8,128)} %get-tuple-element.81), channel_id=1, source_target_pairs={{4,0},{8,4},{12,8},{16,12},{20,16},{24,20},{28,24},{5,1},{9,5},{13... | collective-permute-start | bytes 1572872 | tf_op jit(solution)/shard_map/ppermute | solution.py:279
  4.3 26.9 %collective-permute-start = (f32[2,256,256]{2,1,0:T(8,128)}, f32[2,256,256]{2,1,0:T(8,128)S(1)}, u32[]{:S(2)}, u32[]{:S(2)}) collective-permute-start(f32[2,256,256]{2,1,0:T(8,128)} %get-tuple-element.81), channel_id=1, source_target_pairs={{1,0},{2,1},{3,2},{5,4},{6,5},{7,6},{9,8},{10,9},{11,10},{13,12},{... | collective-permute-start | bytes 1572872 | tf_op jit(solution)/shard_map/ppermute | solution.py:279
  5.6 25.6 %collective-permute-start.2 = (f32[2,256,256]{2,1,0:T(8,128)}, f32[2,256,256]{2,1,0:T(8,128)S(1)}, u32[]{:S(2)}, u32[]{:S(2)}) collective-permute-start(f32[2,256,256]{2,1,0:T(8,128)} %get-tuple-element.80), channel_id=1, source_target_pairs={{4,0},{8,4},{12,8},{16,12},{20,16},{24,20},{28,24},{5,1},{9,5},{13... | collective-permute-start | bytes 1572872 | tf_op jit(solution)/shard_map/ppermute | solution.py:279
  20.8 10.4 %collective-permute-start.3 = (f32[2,256,256]{2,1,0:T(8,128)S(1)}, f32[2,256,256]{2,1,0:T(8,128)}, u32[]{:S(2)}, u32[]{:S(2)}) collective-permute-start(f32[2,256,256]{2,1,0:T(8,128)S(1)} %collective-permute-done.1.right), channel_id=1, source_target_pairs={{1,0},{2,1},{3,2},{5,4},{6,5},{7,6},{9,8},{10,9},{11,10},{13,12},{... | collective-permute-start | bytes 1572872 | tf_op jit(solution)/shard_map/ppermute | solution.py:279
  41.1 4.0 %collective-permute-start.4 = (f32[2,256,256]{2,1,0:T(8,128)S(1)}, f32[2,256,256]{2,1,0:T(8,128)S(1)}, u32[]{:S(2)}, u32[]{:S(2)}) collective-permute-start(f32[2,256,256]{2,1,0:T(8,128)S(1)} %get-tuple-element.60), channel_id=1, source_target_pairs={{0,1},{1,2},{2,3},{4,5},{5,6},{6,7},{8,9},{9,10},{10,11},{12,13},{... | collective-permute-start | bytes 1572872 | tf_op jit(solution)/shard_map/ppermute | solution.py:279
  45.2 12.2 %collective-permute-start.5 = (f32[1024,256]{1,0:T(8,128)S(1)}, f32[1024,256]{1,0:T(8,128)S(1)}, u32[]{:S(2)}, u32[]{:S(2)}) collective-permute-start(f32[1024,256]{1,0:T(8,128)S(1)} %get-tuple-element.62), channel_id=1, source_target_pairs={{0,1},{1,0},{2,3},{3,2},{4,5},{5,4},{6,7},{7,6},{8,9},{9,8},{10,11... | collective-permute-start | bytes 3145736 | tf_op jit(solution)/shard_map/ppermute | solution.py:296
  54.3 27.2 %collective-permute-start.7 = (f32[2,256,256]{2,1,0:T(8,128)S(1)}, f32[2,256,256]{2,1,0:T(8,128)S(1)}, u32[]{:S(2)}, u32[]{:S(2)}) collective-permute-start(f32[2,256,256]{2,1,0:T(8,128)S(1)} %get-tuple-element.65), channel_id=1, source_target_pairs={{0,4},{4,8},{8,12},{12,16},{16,20},{20,24},{24,28},{1,5},{5,9},{9,... | collective-permute-start | bytes 1572872 | tf_op jit(solution)/shard_map/ppermute | solution.py:279
  57.6 23.9 %collective-permute-start.6 = (f32[512,256]{1,0:T(8,128)S(1)}, f32[512,256]{1,0:T(8,128)S(1)}, u32[]{:S(2)}, u32[]{:S(2)}) collective-permute-start(f32[512,256]{1,0:T(8,128)S(1)} %get-tuple-element.64), channel_id=1, source_target_pairs={{0,2},{1,3},{2,0},{3,1},{4,6},{5,7},{6,4},{7,5},{8,10},{9,11},{10,... | collective-permute-start | bytes 1572872 | tf_op jit(solution)/shard_map/ppermute | solution.py:296
  60.0 61.9 %collective-permute-start.17 = (f32[2,256,256]{2,1,0:T(8,128)S(1)}, f32[2,256,256]{2,1,0:T(8,128)S(1)}, u32[]{:S(2)}, u32[]{:S(2)}) collective-permute-start(f32[2,256,256]{2,1,0:T(8,128)S(1)} %get-tuple-element.75), channel_id=1, source_target_pairs={{0,1},{1,2},{2,3},{4,5},{5,6},{6,7},{8,9},{9,10},{10,11},{12,13},{... | collective-permute-start | bytes 1572872 | tf_op jit(solution)/shard_map/ppermute | solution.py:279
  61.9 60.0 %collective-permute-start.16 = (f32[2,256,256]{2,1,0:T(8,128)S(1)}, f32[2,256,256]{2,1,0:T(8,128)S(1)}, u32[]{:S(2)}, u32[]{:S(2)}) collective-permute-start(f32[2,256,256]{2,1,0:T(8,128)S(1)} %add.19), channel_id=1, source_target_pairs={{0,4},{4,8},{8,12},{12,16},{16,20},{20,24},{24,28},{1,5},{5,9},{9,... | collective-permute-start | bytes 1572872 | tf_op jit(solution)/shard_map/ppermute | solution.py:279
  81.6 17.0 %collective-permute-start.8 = (f32[128,256]{1,0:T(8,128)S(1)}, f32[128,256]{1,0:T(8,128)S(1)}, u32[]{:S(2)}, u32[]{:S(2)}) collective-permute-start(f32[128,256]{1,0:T(8,128)S(1)} %get-tuple-element.69), channel_id=1, source_target_pairs={{0,4},{1,5},{2,6},{3,7},{4,0},{5,1},{6,2},{7,3},{8,12},{9,13},{10,... | collective-permute-start | bytes 393224 | tf_op jit(solution)/shard_map/ppermute | solution.py:296
  90.1 8.5 %collective-permute-start.9 = (f32[128,256]{1,0:T(8,128)S(1)}, f32[128,256]{1,0:T(8,128)S(1)}, u32[]{:S(2)}, u32[]{:S(2)}) collective-permute-start(f32[128,256]{1,0:T(8,128)S(1)} %get-tuple-element.70), channel_id=1, source_target_pairs={{0,8},{1,9},{2,10},{3,11},{4,12},{5,13},{6,14},{7,15},{8,0},{9,1},... | collective-permute-start | bytes 393224 | tf_op jit(solution)/shard_map/ppermute | solution.py:296
  90.1 8.5 %collective-permute-start.10 = (f32[128,256]{1,0:T(8,128)S(1)}, f32[128,256]{1,0:T(8,128)S(1)}, u32[]{:S(2)}, u32[]{:S(2)}) collective-permute-start(f32[128,256]{1,0:T(8,128)S(1)} %get-tuple-element.71), channel_id=1, source_target_pairs={{0,12},{1,13},{2,14},{3,15},{4,8},{5,9},{6,10},{7,11},{8,4},{9,5},... | collective-permute-start | bytes 393224 | tf_op jit(solution)/shard_map/ppermute | solution.py:296
  98.6 5.2 %collective-permute-start.11 = (f32[64,256]{1,0:T(8,128)S(1)}, f32[64,256]{1,0:T(8,128)S(1)}, u32[]{:S(2)}, u32[]{:S(2)}) collective-permute-start(f32[64,256]{1,0:T(8,128)S(1)} %get-tuple-element.73), channel_id=1, source_target_pairs={{0,16},{1,17},{2,18},{3,19},{4,20},{5,21},{6,22},{7,23},{8,24},{9,... | collective-permute-start | bytes 196616 | tf_op jit(solution)/shard_map/ppermute | solution.py:296
  103.8 5.2 %collective-permute-start.12 = (f32[64,256]{1,0:T(8,128)S(1)}, f32[64,256]{1,0:T(8,128)S(1)}, u32[]{:S(2)}, u32[]{:S(2)}) collective-permute-start(f32[64,256]{1,0:T(8,128)S(1)} %add_parts.7.refs_0_), channel_id=1, source_target_pairs={{0,16},{1,17},{2,18},{3,19},{4,20},{5,21},{6,22},{7,23},{8,24},{9,... | collective-permute-start | bytes 196616 | tf_op jit(solution)/shard_map/ppermute | solution.py:296
  109.1 9.6 %collective-permute-start.15 = (f32[128,256]{1,0:T(8,128)S(1)}, f32[128,256]{1,0:T(8,128)S(1)}, u32[]{:S(2)}, u32[]{:S(2)}) collective-permute-start(f32[128,256]{1,0:T(8,128)S(1)} %join_parts.3.refs_0_), channel_id=1, source_target_pairs={{0,12},{1,13},{2,14},{3,15},{4,8},{5,9},{6,10},{7,11},{8,4},{9,5},... | collective-permute-start | bytes 393224 | tf_op jit(solution)/shard_map/ppermute | solution.py:296
  115.3 6.0 %collective-permute-start.14 = (f32[128,256]{1,0:T(8,128)S(1)}, f32[128,256]{1,0:T(8,128)S(1)}, u32[]{:S(2)}, u32[]{:S(2)}) collective-permute-start(f32[128,256]{1,0:T(8,128)S(1)} %join_parts.3.refs_0_), channel_id=1, source_target_pairs={{0,8},{1,9},{2,10},{3,11},{4,12},{5,13},{6,14},{7,15},{8,0},{9,1},... | collective-permute-start | bytes 393224 | tf_op jit(solution)/shard_map/ppermute | solution.py:296
  116.9 5.0 %collective-permute-start.13 = (f32[128,256]{1,0:T(8,128)S(1)}, f32[128,256]{1,0:T(8,128)S(1)}, u32[]{:S(2)}, u32[]{:S(2)}) collective-permute-start(f32[128,256]{1,0:T(8,128)S(1)} %join_parts.3.refs_0_), channel_id=1, source_target_pairs={{0,4},{1,5},{2,6},{3,7},{4,0},{5,1},{6,2},{7,3},{8,12},{9,13},{10,... | collective-permute-start | bytes 393224 | tf_op jit(solution)/shard_map/ppermute | solution.py:296
  121.9 11.3 %collective-permute-start.18 = (f32[512,256]{1,0:T(8,128)S(1)}, f32[512,256]{1,0:T(8,128)S(1)}, u32[]{:S(2)}, u32[]{:S(2)}) collective-permute-start(f32[512,256]{1,0:T(8,128)S(1)} %join_parts.4.refs_0_), channel_id=1, source_target_pairs={{0,2},{1,3},{2,0},{3,1},{4,6},{5,7},{6,4},{7,5},{8,10},{9,11},{10,... | collective-permute-start | bytes 1572872 | tf_op jit(solution)/shard_map/ppermute | solution.py:296
  124.8 9.7 %collective-permute-start.19 = (f32[512,256]{1,0:T(8,128)S(1)}, f32[512,256]{1,0:T(8,128)S(1)}, u32[]{:S(2)}, u32[]{:S(2)}) collective-permute-start(f32[512,256]{1,0:T(8,128)S(1)} %join_parts.4.refs_0_), channel_id=1, source_target_pairs={{0,1},{1,0},{2,3},{3,2},{4,5},{5,4},{6,7},{7,6},{8,9},{9,8},{10,11... | collective-permute-start | bytes 1572872 | tf_op jit(solution)/shard_map/ppermute | solution.py:296
  133.3 1.9 %collective-permute-start.20 = (f32[512,256]{1,0:T(8,128)S(1)}, f32[512,256]{1,0:T(8,128)S(1)}, u32[]{:S(2)}, u32[]{:S(2)}) collective-permute-start(f32[512,256]{1,0:T(8,128)S(1)} %collective-permute-done.18.refs_1_), channel_id=1, source_target_pairs={{0,1},{1,0},{2,3},{3,2},{4,5},{5,4},{6,7},{7,6},{8,9},{9,8},{10,11... | collective-permute-start | bytes 1572872 | tf_op jit(solution)/shard_map/ppermute | solution.py:296
